TPU v7x, 256 devices: a whole 4x4x8 slice. The times are simulated.
256 devices in a mesh: band: 32 (over z, y_hi, core), col: 8 (over x, y_lo).
Axes of the slice: x: 4, y: 4 (y_hi: 2, y_lo: 2; y = y_hi * 2 + y_lo), z: 8, core: 2. Of those that a mesh axis runs over, the one named last changes fastest.
Arguments:
- valence: bfloat16 [8, 64, 64, 128], P('col'), may hold values from -6 to 6
- conduction: bfloat16 [128, 64, 64, 128], P('band'), may hold values from -6 to 6
- energy_valence: float32 [8], P('col'), may hold values from -6 to -1
- energy_conduction: float32 [128], P('band'), may hold values from 0.5 to 6
- occ_valence: int32 [8], P('col'), may hold values from 1 to 2
- occ_conduction: int32 [128], P('band'), may hold values from 0 to 1
- gvec_index: int32 [10240], replicated, may hold values from 0 to 262143, as said below
Outputs:
- chi_zero: float32 [2, 10240, 10240], P(None, 'band', 'col')
Inputs may be any that keep to these rules, and one draw needn't show every extreme that they name: `gvec_index`: distinct indices of the 10240 grid points with the shortest wave vectors, where index x * 64 * 64 + y * 64 + z stands for the vector with components ((x + 32) mod 64) - 32 and so on; ordered by length, equal lengths in any order.
All inputs are finite; a program needn't handle non-finite values.
Results may differ from a plain program's by a relative error of at most 0.01.
Values may be sent and summed in bfloat16 or wider, within the bound.
No kernel may reach another device: no remote copies, remote signals or barrier semaphores. Data moves between devices by JAX's collectives and lax.ppermute only.
A program may use at most 320 MiB of HBM per device.

v0:
```python
import functools
import math

import jax
import jax.numpy as jnp
import numpy as np
from jax import lax
from jax.experimental import pallas as pl
from jax.experimental.pallas import tpu as pltpu
from jax.sharding import PartitionSpec as P
from ml_dtypes import bfloat16

NG = 64
NPW = 10240


def sphere_radius():
    axis = (np.arange(NG) + NG // 2) % NG - NG // 2
    square = axis * axis
    length = np.sort((square[:, None, None] + square[None, :, None] + square[None, None, :]).ravel())
    return int(length[NPW - 1])


LIMIT = sphere_radius()
KMAX = math.isqrt(LIMIT)
KS = list(range(-KMAX, KMAX + 1))
NK = len(KS)
YORDER = [0]
for step in range(1, KMAX + 1):
    YORDER += [step, -step]
NY = -(-len(YORDER) // 8) * 8
YORDER += [0] * (NY - len(YORDER))


def rows_for(kx):
    return -(-(2 * math.isqrt(LIMIT - kx * kx) + 1) // 8) * 8


BASE = []
total = 0
for kx in KS:
    BASE.append(total)
    total += rows_for(kx)
USED_ROWS = total
ROWS = -(-total // 256) * 256


def cos_sin(freqs):
    product = np.asarray(freqs)[:, None] * np.arange(NG)[None, :] % NG
    angle = (2.0 * math.pi / NG) * product
    scale = 1.0 / math.sqrt(NG)
    return np.cos(angle) * scale, np.sin(angle) * scale


def x_matrix():
    cos, sin = cos_sin(KS)
    eye = np.eye(8)
    return np.concatenate([np.kron(cos, eye), np.kron(sin, eye)], axis=0).astype(bfloat16)


def y_matrix():
    cos, sin = cos_sin(YORDER)
    return np.concatenate([cos, sin], axis=0).astype(bfloat16)


def z_matrix(pairs):
    cos, sin = cos_sin(KS)
    out = np.zeros((NK, 2, pairs, pairs, 2, NG), np.float64)
    for p in range(pairs):
        out[:, 0, p, p, 0] = cos
        out[:, 0, p, p, 1] = sin
        out[:, 1, p, p, 0] = -sin
        out[:, 1, p, p, 1] = cos
    return out.reshape(NK * 2 * pairs, pairs * 2 * NG).astype(bfloat16)


def signed(index):
    return ((index + NG // 2) & (NG - 1)) - NG // 2


def density_kernel(
    pairs, dests, col_width, row_width,
    v_ref, c_ref, xm_ref, ym_ref, zm_ref, g_ref, ev_ref, ec_ref, ov_ref, oc_ref,
    rho_ref, row_ref,
    first_ref, second_ref, pos_ref, kz_ref, flat_ref,
):
    step = pl.program_id(0)
    lanes = pairs * 2 * NG
    lane = lax.broadcasted_iota(jnp.int32, (1, 1, 2 * NG), 2)
    low = lane < NG
    field_v = v_ref[0].astype(jnp.float32)
    turned = pltpu.roll(field_v, NG, 2)
    v_re = jnp.where(low, field_v, turned)
    v_im = jnp.where(low, turned, -field_v)
    parts = []
    for p in range(pairs):
        field_c = c_ref[p].astype(jnp.float32)
        parts.append(v_re * field_c + v_im * pltpu.roll(field_c, NG, 2))
    sign = jnp.where(lax.broadcasted_iota(jnp.int32, (1, 2 * NG), 1) < NG, 1.0, -1.0)

    def combine(both, rows):
        cols = []
        for p in range(pairs):
            take = slice(p * 2 * NG, (p + 1) * 2 * NG)
            cols.append(both[:rows, take] + sign * pltpu.roll(both[rows : 2 * rows, take], NG, 1))
        return jnp.concatenate(cols, axis=1)

    halves = []
    for half in range(2):
        stacked = jnp.concatenate(
            [
                part[:, half * 8 : half * 8 + 8].reshape(NG * 8, 2 * NG).astype(jnp.bfloat16)
                for part in parts
            ],
            axis=1,
        )
        both = jnp.dot(xm_ref[...], stacked, preferred_element_type=jnp.float32)
        halves.append(combine(both, NK * 8).reshape(NK, 8, lanes))
    merged = jnp.concatenate(halves, axis=1).astype(jnp.bfloat16)
    first_ref[:, pl.ds(pl.multiple_of(step * 16, 16), 16), :] = merged

    @pl.when(step == pl.num_programs(0) - 1)
    def _():
        second_ref[USED_ROWS:, :] = jnp.zeros((ROWS - USED_ROWS, lanes), jnp.float32)
        for i, kx in enumerate(KS):
            both = jnp.dot(ym_ref[...], first_ref[i], preferred_element_type=jnp.float32)
            second_ref[BASE[i] : BASE[i] + rows_for(kx), :] = combine(both, NY)[: rows_for(kx)]
        second = second_ref[...].astype(jnp.bfloat16)
        third = lax.dot_general(
            zm_ref[...], second, (((1,), (1,)), ((), ())), preferred_element_type=jnp.float32
        ).astype(jnp.bfloat16)
        index = g_ref[...]
        comp_x = signed(index >> 12)
        comp_y = signed((index >> 6) & (NG - 1))
        place = 2 * jnp.abs(comp_y) - (comp_y > 0).astype(jnp.int32)
        for i, kx in enumerate(KS):
            place = jnp.where(comp_x == kx, place + BASE[i], place)
        pos_ref[...] = place
        kz_ref[...] = signed(index & (NG - 1)) + KMAX
        row_id = lax.broadcasted_iota(jnp.int32, (ROWS, 256), 0)
        blocks = col_width // 256

        def body(dest, carry):
            for k in range(blocks):
                which = dest * blocks + k
                pos = pos_ref[pl.ds(which, 1), :]
                kz = kz_ref[pl.ds(which, 1), :]
                pick = jnp.where(row_id == pos, 1.0, 0.0).astype(jnp.bfloat16)
                found = jnp.dot(third, pick, preferred_element_type=jnp.float32)
                found = found.reshape(NK, 2 * pairs, 256)
                acc = jnp.zeros((2 * pairs, 256), jnp.float32)
                for i in range(NK):
                    acc = jnp.where(kz == i, found[i], acc)
                rho_ref[dest, :, k * 256 : (k + 1) * 256] = acc.astype(jnp.bfloat16)
                flat_ref[which] = acc
            return carry

        lax.fori_loop(0, dests, body, 0)
        which_pair = lax.broadcasted_iota(jnp.int32, (2 * pairs, 128), 0) % pairs
        occ_diff = jnp.zeros((2 * pairs, 128), jnp.float32)
        energy = jnp.ones((2 * pairs, 128), jnp.float32)
        for p in range(pairs):
            occ_diff = jnp.where(which_pair == p, (ov_ref[0] - oc_ref[p]).astype(jnp.float32), occ_diff)
            energy = jnp.where(which_pair == p, ev_ref[0] - ec_ref[p], energy)
        weight = (occ_diff / energy / math.sqrt(1024))[:, :1]
        group = math.lcm(row_width, 256)

        def row_body(block, carry):
            wide = jnp.concatenate(
                [flat_ref[block * (group // 256) + k] for k in range(group // 256)], axis=1
            )
            wide = (wide * weight).astype(jnp.bfloat16).astype(jnp.float32)
            for k in range(group // row_width):
                row_ref[block * (group // row_width) + k] = wide[
                    :, k * row_width : (k + 1) * row_width
                ].astype(jnp.bfloat16)
            return carry

        lax.fori_loop(0, NPW // group, row_body, 0)


def densities(valence, conduction, energy_valence, energy_conduction, occ_valence, occ_conduction, gvec_index, n_col, n_band):
    pairs = conduction.shape[0]
    lanes = pairs * 2 * NG
    col_width = NPW // n_col
    row_width = NPW // n_band
    smem = pl.BlockSpec(memory_space=pltpu.SMEM)
    whole = lambda shape: pl.BlockSpec(shape, lambda s: (0,) * len(shape))
    xm, ym, zm = x_matrix(), y_matrix(), z_matrix(pairs)
    return pl.pallas_call(
        functools.partial(density_kernel, pairs, n_col, col_width, row_width),
        grid=(NG // 16,),
        in_specs=[
            pl.BlockSpec((1, NG, 16, 2 * NG), lambda s: (0, 0, s, 0)),
            pl.BlockSpec((pairs, NG, 16, 2 * NG), lambda s: (0, 0, s, 0)),
            whole(xm.shape), whole(ym.shape), whole(zm.shape),
            whole((NPW // 256, 256)),
            smem, smem, smem, smem,
        ],
        out_specs=[whole((n_col, 2 * pairs, col_width)), whole((n_band, 2 * pairs, row_width))],
        out_shape=[
            jax.ShapeDtypeStruct((n_col, 2 * pairs, col_width), jnp.bfloat16),
            jax.ShapeDtypeStruct((n_band, 2 * pairs, row_width), jnp.bfloat16),
        ],
        scratch_shapes=[
            pltpu.VMEM((NK, NG, lanes), jnp.bfloat16),
            pltpu.VMEM((ROWS, lanes), jnp.float32),
            pltpu.VMEM((NPW // 256, 256), jnp.int32),
            pltpu.VMEM((NPW // 256, 256), jnp.int32),
            pltpu.VMEM((NPW // 256, 2 * pairs, 256), jnp.float32),
        ],
        compiler_params=pltpu.CompilerParams(vmem_limit_bytes=48 * 1024 * 1024),
        cost_estimate=pl.CostEstimate(flops=2 * 10**9, bytes_accessed=6 * 10**6, transcendentals=0),
    )(
        valence, conduction, jnp.asarray(xm), jnp.asarray(ym), jnp.asarray(zm),
        gvec_index.reshape(NPW // 256, 256),
        energy_valence, energy_conduction, occ_valence, occ_conduction,
    )


def contract_kernel(n_bands, r_ref, c_ref, out_ref, lhs_ref):
    step = pl.program_id(0)
    width = r_ref.shape[-1]

    @pl.when(step == 0)
    def _():
        rows = r_ref[...]
        nv, nb, po, _ = rows.shape
        f = rows.astype(jnp.float32)
        half = po // 2
        swapped = jnp.concatenate([f[:, :, half:], -f[:, :, :half]], axis=2)
        for v in range(nv):
            for src, which in ((f, 0), (swapped, 1)):
                lhs_ref[v, which * width : (which + 1) * width, :] = (
                    src[v].reshape(nb * po, width).T.astype(jnp.bfloat16)
                )

    tile = c_ref.shape[-1]
    nv = lhs_ref.shape[0]
    nb, _, po, _ = c_ref.shape
    acc = jnp.zeros((2 * width, tile), jnp.float32)
    for v in range(nv):
        cols = c_ref[:, v].astype(jnp.float32).reshape(nb * po, tile).astype(jnp.bfloat16)
        acc += jnp.dot(lhs_ref[v], cols, preferred_element_type=jnp.float32)
    out_ref[...] = acc.reshape(2, width, tile)


def contract(rows, cols):
    nv, nb, po, width = rows.shape
    total = cols.shape[-1]
    tile = 256
    return pl.pallas_call(
        functools.partial(contract_kernel, nb),
        grid=(total // tile,),
        in_specs=[
            pl.BlockSpec(rows.shape, lambda s: (0, 0, 0, 0)),
            pl.BlockSpec((nb, nv, po, tile), lambda s: (0, 0, 0, s)),
        ],
        out_specs=pl.BlockSpec((2, width, tile), lambda s: (0, 0, s)),
        out_shape=jax.ShapeDtypeStruct((2, width, total), jnp.float32),
        scratch_shapes=[pltpu.VMEM((nv, 2 * width, nb * po), jnp.bfloat16)],
        compiler_params=pltpu.CompilerParams(vmem_limit_bytes=48 * 1024 * 1024),
        cost_estimate=pl.CostEstimate(
            flops=4 * nv * nb * po * width * total, bytes_accessed=10**7, transcendentals=0
        ),
    )(rows, cols)


def local(
    valence, conduction, energy_valence, energy_conduction, occ_valence, occ_conduction, gvec_index
):
    n_col, n_band = lax.axis_size("col"), lax.axis_size("band")
    pairs = conduction.shape[0]
    rho, weighted = densities(
        valence, conduction, energy_valence, energy_conduction, occ_valence, occ_conduction,
        gvec_index, n_col, n_band,
    )
    cols = lax.all_to_all(rho, "col", split_axis=0, concat_axis=0, tiled=True)
    rows = lax.all_to_all(weighted, "band", split_axis=0, concat_axis=0, tiled=True)
    cols = lax.all_gather(cols, "band", axis=0)
    rows = lax.all_gather(rows, "col", axis=0)
    return contract(rows, cols)


def solution(mesh):
    return jax.shard_map(
        local,
        mesh=mesh,
        in_specs=(
            P("col", None, None, None),
            P("band", None, None, None),
            P("col"),
            P("band"),
            P("col"),
            P("band"),
            P(),
        ),
        out_specs=P(None, "band", "col"),
        check_vma=False,
    )
```

profile of v0, /device:TPU:1, one launch (start us, length us, event | category | flops | bytes accessed | tf_op | source)
XLA Modules:
  0.0 203.6 jit_solution(17582906786221387006)
XLA Ops:
  6.5 0.0 all-gather.5.cloned.1.call-start
  7.8 0.8 reshape.3.g_ref
  8.6 0.0 copy-start.1
  8.6 1.2 copy-done.1
  9.9 0.0 copy-start.2
  9.9 0.7 copy-done.2
  10.5 0.0 copy-start.3
  10.5 0.7 copy-done.3
  11.2 0.0 copy-start.4
  11.2 1.0 copy-done.4
  12.2 0.0 copy-start.5
  12.2 0.9 copy-done.5
  13.1 0.0 copy-start.6
  13.1 0.7 copy-done.6
  13.8 13.5 %shard_map.100 = (bf16[8,8,1280]{2,1,0:T(8,128)(2,1)S(1)}, bf16[32,8,320]{2,1,0:T(8,128)(2,1)S(1)}) custom-call(bf16[1,64,64,128]{3,2,1,0:T(8,128)(2,1)S(1)} %copy-done.1, bf16[4,64,64,128]{3,2,1,0:T(8,128)(2,1)} %c_ref.1, bf16[432,512]{1,0:T(8,128)(2,1)S(1)} %copy-done.4, bf16[64,64]{1,0:T(8,128)(2,1)S(1)} %copy-done.6, bf16[216,512]{1,0:T(8,128)(2,1)S(1)} %copy-done.5, ...), custom_call_target="tpu_custom_call" | custom-call | flops 2000000000 | bytes 6000000 | tf_op jit(solution)/shard_map/pallas_call | solution.py:190
  27.3 24.5 %all_to_all.10 = bf16[32,8,320]{2,1,0:T(8,128)(2,1)} all-to-all(bf16[32,8,320]{2,1,0:T(8,128)(2,1)S(1)} %get-tuple-element.7), channel_id=1, replica_groups=mesh['band'=32,'col'=8] {'band'}, dimensions={0} | all-to-all | bytes 327680 | tf_op jit(solution)/shard_map/all_to_all | solution.py:279
  51.8 0.0 all-gather.5.cloned.1.call-update
  51.8 0.0 all-gather.7.cloned.1.call-start
  51.9 9.7 %all_to_all.11 = bf16[8,8,1280]{2,1,0:T(8,128)(2,1)} all-to-all(bf16[8,8,1280]{2,1,0:T(8,128)(2,1)S(1)} %get-tuple-element.8), channel_id=1, replica_groups=mesh['band'=32,'col'=8] {'col'}, dimensions={0} | all-to-all | bytes 327680 | tf_op jit(solution)/shard_map/all_to_all | solution.py:278
  61.6 0.0 all-gather.7.cloned.1.call-update
  61.7 29.3 %all-gather.5.cloned.1.call-done = bf16[256,8,320]{2,1,0:T(8,128)(2,1)} async-done(((bf16[32,8,320]{2,1,0:T(8,128)(2,1)}), bf16[256,8,320]{2,1,0:T(8,128)(2,1)}) %all-gather.5.cloned.1.call-update) | async-done | bytes 1310736 | tf_op jit(solution)/shard_map/all_gather | solution.py:281
  90.9 95.9 %all-gather.7.cloned.1.call-done = bf16[256,8,1280]{2,1,0:T(8,128)(2,1)} async-done(((bf16[8,8,1280]{2,1,0:T(8,128)(2,1)}), bf16[256,8,1280]{2,1,0:T(8,128)(2,1)}) %all-gather.7.cloned.1.call-update) | async-done | bytes 5242896 | tf_op jit(solution)/shard_map/all_gather | solution.py:280
  186.9 0.0 copy-start
  186.9 1.4 copy-done
  188.3 8.5 %shard_map.101 = f32[2,320,1280]{2,1,0:T(8,128)} custom-call(bf16[8,32,8,320]{3,2,1,0:T(8,128)(2,1)S(1)} %bitcast.2, bf16[32,8,8,1280]{3,2,1,0:T(8,128)(2,1)} %bitcast.3), custom_call_target="tpu_custom_call" | custom-call | flops 3355443200 | bytes 10000000 | tf_op jit(solution)/shard_map/pallas_call | solution.py:252
Async XLA Ops:
  6.5 84.4 %all-gather.5.cloned.1.call-start = ((), (), s32[]{:S(2)}) async-start(), calls=%async_computation.2 | async-start | bytes 1769472 | tf_op jit(solution)/shard_map/all_gather | solution.py:281
  8.6 1.2 copy-start.1
  9.9 0.7 copy-start.2
  10.5 0.7 copy-start.3
  11.2 1.0 copy-start.4
  12.2 0.9 copy-start.5
  13.1 0.7 copy-start.6
  51.8 135.0 %all-gather.7.cloned.1.call-start = ((), (), s32[]{:S(2)}) async-start(), calls=%async_computation.3 | async-start | bytes 5406720 | tf_op jit(solution)/shard_map/all_gather | solution.py:280
  186.9 1.4 copy-start
Sparse Core Ops, SparseCore 0:
  52.0 38.9 all-gather.4
  93.7 93.1 all-gather.6
where the time goes:
time: 204 us
  waiting for transfers between devices  125 us (61%)
  blocking collectives  34.2 us (17%)
  Pallas kernels  22 us (11%)
  between operations  14.7 us (7%)
  local copies, waits for them, and re-layouts  7.39 us (4%)
    all_gather x1, waiting for transfers between devices, local(): cols = lax.all_gather(cols, 'band', axis=0)  95.9 us
    all_gather x1, waiting for transfers between devices, local(): rows = lax.all_gather(rows, 'col', axis=0)  29.3 us
    all_to_all x1, blocking collectives, local(): lax.all_to_all(weighted, 'band', split_axis=0, concat_axis=0, tiled=True)  24.5 us
    pallas_call x1, Pallas kernels, densities(): pl.pallas_call(functools.partial(density_kernel, pairs, n_col, col_width,...  13.5 us
    all_to_all x1, blocking collectives, local(): cols = lax.all_to_all(rho, 'col', split_axis=0, concat_axis=0, tiled=True)  9.74 us
    pallas_call x1, Pallas kernels, contract(): pl.pallas_call(functools.partial(contract_kernel, nb), grid=(total // til...  8.52 us
    unnamed x14, local copies, waits for them, and re-layouts  6.6 us
  transfers between devices with their start and end apart: 2, of which 2 were waited for; matrix products, arithmetic and copies ran while one was open for 0% of the time, Pallas kernels for 0%

commit v1 on v0

--- a/solution.py
+++ b/solution.py
@@ -12,6 +12,10 @@
 
 NG = 64
 NPW = 10240
+QUAD = 4
+TILE = 256
+VMEM_LIMIT = 60 * 1024 * 1024
+SMALL_LIMIT = 16 * 1024 * 1024
 
 
 def sphere_radius():
@@ -79,9 +83,9 @@
 
 
 def density_kernel(
-    pairs, dests, col_width, row_width,
+    pairs, dests, col_width,
     v_ref, c_ref, xm_ref, ym_ref, zm_ref, g_ref, ev_ref, ec_ref, ov_ref, oc_ref,
-    rho_ref, row_ref,
+    rho_ref, weighted_ref,
     first_ref, second_ref, pos_ref, kz_ref, flat_ref,
 ):
     step = pl.program_id(0)
@@ -163,32 +167,25 @@
             occ_diff = jnp.where(which_pair == p, (ov_ref[0] - oc_ref[p]).astype(jnp.float32), occ_diff)
             energy = jnp.where(which_pair == p, ev_ref[0] - ec_ref[p], energy)
         weight = (occ_diff / energy / math.sqrt(1024))[:, :1]
-        group = math.lcm(row_width, 256)
-
-        def row_body(block, carry):
-            wide = jnp.concatenate(
-                [flat_ref[block * (group // 256) + k] for k in range(group // 256)], axis=1
-            )
-            wide = (wide * weight).astype(jnp.bfloat16).astype(jnp.float32)
-            for k in range(group // row_width):
-                row_ref[block * (group // row_width) + k] = wide[
-                    :, k * row_width : (k + 1) * row_width
-                ].astype(jnp.bfloat16)
+
+        def weigh(dest, carry):
+            for k in range(blocks):
+                wide = flat_ref[dest * blocks + k] * weight
+                weighted_ref[dest, :, k * 256 : (k + 1) * 256] = wide.astype(jnp.bfloat16)
             return carry
 
-        lax.fori_loop(0, NPW // group, row_body, 0)
-
-
-def densities(valence, conduction, energy_valence, energy_conduction, occ_valence, occ_conduction, gvec_index, n_col, n_band):
+        lax.fori_loop(0, dests, weigh, 0)
+
+
+def densities(valence, conduction, energy_valence, energy_conduction, occ_valence, occ_conduction, gvec_index, n_col):
     pairs = conduction.shape[0]
     lanes = pairs * 2 * NG
     col_width = NPW // n_col
-    row_width = NPW // n_band
     smem = pl.BlockSpec(memory_space=pltpu.SMEM)
     whole = lambda shape: pl.BlockSpec(shape, lambda s: (0,) * len(shape))
     xm, ym, zm = x_matrix(), y_matrix(), z_matrix(pairs)
     return pl.pallas_call(
-        functools.partial(density_kernel, pairs, n_col, col_width, row_width),
+        functools.partial(density_kernel, pairs, n_col, col_width),
         grid=(NG // 16,),
         in_specs=[
             pl.BlockSpec((1, NG, 16, 2 * NG), lambda s: (0, 0, s, 0)),
@@ -197,11 +194,8 @@
             whole((NPW // 256, 256)),
             smem, smem, smem, smem,
         ],
-        out_specs=[whole((n_col, 2 * pairs, col_width)), whole((n_band, 2 * pairs, row_width))],
-        out_shape=[
-            jax.ShapeDtypeStruct((n_col, 2 * pairs, col_width), jnp.bfloat16),
-            jax.ShapeDtypeStruct((n_band, 2 * pairs, row_width), jnp.bfloat16),
-        ],
+        out_specs=[whole((n_col, 2 * pairs, col_width))] * 2,
+        out_shape=[jax.ShapeDtypeStruct((n_col, 2 * pairs, col_width), jnp.bfloat16)] * 2,
         scratch_shapes=[
             pltpu.VMEM((NK, NG, lanes), jnp.bfloat16),
             pltpu.VMEM((ROWS, lanes), jnp.float32),
@@ -209,7 +203,7 @@
             pltpu.VMEM((NPW // 256, 256), jnp.int32),
             pltpu.VMEM((NPW // 256, 2 * pairs, 256), jnp.float32),
         ],
-        compiler_params=pltpu.CompilerParams(vmem_limit_bytes=48 * 1024 * 1024),
+        compiler_params=pltpu.CompilerParams(vmem_limit_bytes=VMEM_LIMIT),
         cost_estimate=pl.CostEstimate(flops=2 * 10**9, bytes_accessed=6 * 10**6, transcendentals=0),
     )(
         valence, conduction, jnp.asarray(xm), jnp.asarray(ym), jnp.asarray(zm),
@@ -218,68 +212,207 @@
     )
 
 
-def contract_kernel(n_bands, r_ref, c_ref, out_ref, lhs_ref):
-    step = pl.program_id(0)
-    width = r_ref.shape[-1]
-
-    @pl.when(step == 0)
-    def _():
-        rows = r_ref[...]
-        nv, nb, po, _ = rows.shape
-        f = rows.astype(jnp.float32)
-        half = po // 2
-        swapped = jnp.concatenate([f[:, :, half:], -f[:, :, :half]], axis=2)
-        for v in range(nv):
-            for src, which in ((f, 0), (swapped, 1)):
-                lhs_ref[v, which * width : (which + 1) * width, :] = (
-                    src[v].reshape(nb * po, width).T.astype(jnp.bfloat16)
-                )
-
-    tile = c_ref.shape[-1]
-    nv = lhs_ref.shape[0]
-    nb, _, po, _ = c_ref.shape
-    acc = jnp.zeros((2 * width, tile), jnp.float32)
-    for v in range(nv):
-        cols = c_ref[:, v].astype(jnp.float32).reshape(nb * po, tile).astype(jnp.bfloat16)
-        acc += jnp.dot(lhs_ref[v], cols, preferred_element_type=jnp.float32)
-    out_ref[...] = acc.reshape(2, width, tile)
-
-
-def contract(rows, cols):
-    nv, nb, po, width = rows.shape
-    total = cols.shape[-1]
-    tile = 256
+def split_kernel(x_ref, out0_ref, out1_ref, out2_ref, out3_ref, hold_ref):
+    me = lax.axis_index("band") % QUAD
+    width = out0_ref.shape[-1]
+    for k in range(QUAD):
+        hold_ref[k] = x_ref[:, k * width : (k + 1) * width]
+    for k, ref in enumerate((out0_ref, out1_ref, out2_ref, out3_ref)):
+        ref[...] = hold_ref[me ^ k]
+
+
+def split(x):
+    rows, total = x.shape
     return pl.pallas_call(
-        functools.partial(contract_kernel, nb),
-        grid=(total // tile,),
-        in_specs=[
-            pl.BlockSpec(rows.shape, lambda s: (0, 0, 0, 0)),
-            pl.BlockSpec((nb, nv, po, tile), lambda s: (0, 0, 0, s)),
+        split_kernel,
+        out_shape=[jax.ShapeDtypeStruct((rows, total // QUAD), jnp.bfloat16)] * QUAD,
+        scratch_shapes=[pltpu.VMEM((QUAD, rows, total // QUAD), jnp.bfloat16)],
+        compiler_params=pltpu.CompilerParams(vmem_limit_bytes=SMALL_LIMIT),
+    )(x)
+
+
+def stack_kernel(*refs):
+    for k, ref in enumerate(refs[:-2]):
+        refs[-1][k] = ref[...]
+
+
+def stack(parts, after):
+    vmem = pl.BlockSpec(memory_space=pltpu.VMEM)
+    return pl.pallas_call(
+        stack_kernel,
+        in_specs=[vmem] * len(parts) + [pl.BlockSpec(memory_space=pl.ANY)],
+        out_specs=vmem,
+        out_shape=jax.ShapeDtypeStruct((len(parts),) + parts[0].shape, jnp.bfloat16),
+        compiler_params=pltpu.CompilerParams(vmem_limit_bytes=SMALL_LIMIT),
+    )(*parts, after)
+
+
+def left_kernel(n_col, depth, own_ref, next_ref, prev_ref, high_ref, low_ref, out_ref, hold_ref):
+    col = lax.axis_index("col")
+    plane = lax.axis_index("band") // QUAD
+    xs = n_col // 2
+    x, y = col // 2, col % 2
+
+    def put(source, ref):
+        hold_ref[source] = ref[...].astype(jnp.float32)
+
+    for k in range(2):
+        put(x * 2 + (y ^ k), own_ref.at[k])
+        put((x + xs - 1) % xs * 2 + (y ^ k), next_ref.at[k])
+        put((x + 1) % xs * 2 + (y ^ k), prev_ref.at[k])
+    put((x + 2) % xs * 2 + y, high_ref)
+    put((x + 2) % xs * 2 + (y ^ 1), low_ref)
+    n, quad, rows, width = hold_ref.shape
+    po = rows // depth
+    turns = [0]
+    for step in range(1, depth // 2):
+        turns += [step, depth - step]
+    turns.append(depth // 2)
+    depth_rows = quad * n * po
+    for slot, turn in enumerate(turns):
+        source = pl.multiple_of((plane + depth - turn) % depth * po, po)
+        f = hold_ref[:, :, pl.ds(source, po), :]
+        f = jnp.concatenate([f[:, k] for k in range(quad)], axis=0)
+        swapped = jnp.concatenate([f[:, po // 2 :], -f[:, : po // 2]], axis=1)
+        for which, src in enumerate((f, swapped)):
+            out_ref[which * width : (which + 1) * width, slot * depth_rows : (slot + 1) * depth_rows] = (
+                src.reshape(depth_rows, width).astype(jnp.bfloat16).T
+            )
+
+
+def left(n_col, depth, parts):
+    _, quad, rows, width = parts[0].shape
+    return pl.pallas_call(
+        functools.partial(left_kernel, n_col, depth),
+        out_shape=jax.ShapeDtypeStruct((2 * width, depth * quad * rows), jnp.bfloat16),
+        scratch_shapes=[pltpu.VMEM((n_col, quad, rows, width), jnp.float32)],
+        compiler_params=pltpu.CompilerParams(vmem_limit_bytes=SMALL_LIMIT),
+    )(*parts)
+
+
+def product_on(core, turns, l_ref, blocks, out_ref, out_buf, sem):
+    double = l_ref.shape[0]
+    total = out_ref.shape[-1]
+    slots = len(turns)
+    quarter = l_ref.shape[1] // slots // QUAD
+    copies = []
+    for t in range(total // TILE):
+        take = slice(t * TILE, (t + 1) * TILE)
+        pieces = [None] * (slots * QUAD)
+        at = 0
+        for step, mirrored, count in turns:
+            if step == 0:
+                slot = 0
+            elif 2 * step == slots:
+                slot = slots - 1
+            else:
+                slot = 2 * step - 1 if core == mirrored else 2 * step
+            each = QUAD // count
+            for part in range(count):
+                for k in range(each):
+                    pieces[slot * QUAD + part * each + (k ^ mirrored)] = blocks[at + part][
+                        k * quarter : (k + 1) * quarter, take
+                    ]
+            at += count
+        tile = jnp.dot(
+            l_ref[...], jnp.concatenate(pieces, axis=0), preferred_element_type=jnp.float32
+        )
+        out_buf[:, :, take] = tile.reshape(2, double // 2, TILE)
+        copy = pltpu.make_async_copy(out_buf.at[:, :, take], out_ref.at[:, :, take], sem.at[t])
+        copy.start()
+        copies.append(copy)
+    for copy in copies:
+        copy.wait()
+
+
+def product_kernel(turns, l_ref, *refs):
+    out_ref, out_buf, sem = refs[-3:]
+    core = lax.axis_index("band") % 2
+    for which in range(2):
+        pl.when(core == which)(
+            functools.partial(
+                product_on, which, turns, l_ref, refs[:-3], out_ref, out_buf, sem
+            )
+        )
+
+
+def product(lhs, groups):
+    double, all_rows = lhs.shape
+    blocks = [b for g in groups for b in g[2]]
+    total = blocks[0].shape[1]
+    vmem = pl.BlockSpec(memory_space=pltpu.VMEM)
+    return pl.pallas_call(
+        functools.partial(product_kernel, [g[:2] + (len(g[2]),) for g in groups]),
+        in_specs=[vmem] * (1 + len(blocks)),
+        out_specs=pl.BlockSpec(memory_space=pl.ANY),
+        out_shape=jax.ShapeDtypeStruct((2, double // 2, total), jnp.float32),
+        scratch_shapes=[
+            pltpu.VMEM((2, double // 2, total), jnp.float32),
+            pltpu.SemaphoreType.DMA((total // TILE,)),
         ],
-        out_specs=pl.BlockSpec((2, width, tile), lambda s: (0, 0, s)),
-        out_shape=jax.ShapeDtypeStruct((2, width, total), jnp.float32),
-        scratch_shapes=[pltpu.VMEM((nv, 2 * width, nb * po), jnp.bfloat16)],
-        compiler_params=pltpu.CompilerParams(vmem_limit_bytes=48 * 1024 * 1024),
-        cost_estimate=pl.CostEstimate(
-            flops=4 * nv * nb * po * width * total, bytes_accessed=10**7, transcendentals=0
-        ),
-    )(rows, cols)
+        compiler_params=pltpu.CompilerParams(vmem_limit_bytes=SMALL_LIMIT),
+    )(lhs, *blocks)
+
+
+def permute(x, n_band, n_col, move):
+    pairs = []
+    for band in range(n_band):
+        for col in range(n_col):
+            to_band, to_col = move(band, col)
+            pairs.append((band * n_col + col, to_band * n_col + to_col))
+    return lax.ppermute(x, ("band", "col"), pairs)
 
 
 def local(
     valence, conduction, energy_valence, energy_conduction, occ_valence, occ_conduction, gvec_index
 ):
     n_col, n_band = lax.axis_size("col"), lax.axis_size("band")
-    pairs = conduction.shape[0]
+    depth = n_band // QUAD
+    xs = n_col // 2
+    send = functools.partial(permute, n_band=n_band, n_col=n_col)
+    shift = lambda band, by: (band // QUAD + by) % depth * QUAD + band % QUAD
+    ring = lambda x: send(x, move=lambda b, c: (shift(b, 1 if b % 2 == 0 else -1), c))
+    swap = lambda x: send(x, move=lambda b, c: (b ^ 1, c))
+    high = lambda x: send(x, move=lambda b, c: (b ^ 2, c))
+    along_x = lambda x, by: send(x, move=lambda b, c: (b, (c // 2 + by) % xs * 2 + c % 2))
     rho, weighted = densities(
         valence, conduction, energy_valence, energy_conduction, occ_valence, occ_conduction,
-        gvec_index, n_col, n_band,
+        gvec_index, n_col,
     )
-    cols = lax.all_to_all(rho, "col", split_axis=0, concat_axis=0, tiled=True)
-    rows = lax.all_to_all(weighted, "band", split_axis=0, concat_axis=0, tiled=True)
-    cols = lax.all_gather(cols, "band", axis=0)
-    rows = lax.all_gather(rows, "col", axis=0)
-    return contract(rows, cols)
+    lines = [[z * QUAD + q for z in range(depth)] for q in range(QUAD)]
+    weighted = lax.all_to_all(
+        weighted, "band", split_axis=0, concat_axis=0, tiled=True, axis_index_groups=lines
+    )
+    own = lax.all_to_all(rho, "col", split_axis=0, concat_axis=0, tiled=True)
+    size = own.shape[0] * own.shape[1]
+    own = own.reshape(size, own.shape[2])
+    weighted = weighted.reshape(size, weighted.shape[2])
+
+    across = high(own)
+    near_ring = [jnp.concatenate([own, swap(own)], axis=0)]
+    near_ring.append(ring(near_ring[0]))
+    parts = split(weighted)
+    parts = [parts[0]] + [
+        send(parts[k], move=lambda b, c, k=k: (b ^ k, c)) for k in range(1, QUAD)
+    ]
+    far_ring = [jnp.concatenate([across, swap(across)], axis=0)]
+    far_ring.append(ring(far_ring[0]))
+    near_ring.append(ring(near_ring[1]))
+    mine = stack(parts, near_ring[2])
+    beside = send(mine, move=lambda b, c: (b, c ^ 1))
+    far_ring.append(ring(far_ring[1]))
+    near_ring.append(ring(near_ring[2]))
+    pair = stack([mine, beside], near_ring[3])
+    after, before = along_x(pair, 1), along_x(pair, -1)
+    far_ring.append(ring(far_ring[2]))
+    last = [ring(near_ring[-1][:size]), ring(far_ring[-1][:size])]
+    parts = [pair, after, before, along_x(after[0], 1), along_x(before[1], -1)]
+    groups = [(0, 0, (near_ring[0], far_ring[0]))]
+    for step in range(1, depth // 2):
+        groups.append((step, 0, (near_ring[step], far_ring[step])))
+        groups.append((step, 1, (swap(near_ring[step]), swap(far_ring[step]))))
+    groups.append((depth // 2, 0, (last[0], swap(last[0]), last[1], swap(last[1]))))
+    return product(left(n_col, depth, parts), groups)
 
 
 def solution(mesh):

time: 204 us -> 108 us (0.53)
  waiting for transfers between devices: 125 us -> 22.5 us
  starting transfers between devices: 0.04 us -> 50.1 us
  blocking collectives: 34.2 us -> 11.3 us
  between operations: 14.7 us -> 1.61 us
  local copies, waits for them, and re-layouts: 7.39 us -> 1.49 us
    all_gather x2 -> x0, waiting for transfers between devices: 125 us -> none  [the longest x1 95.9 us: local(): cols = lax.all_gather(cols, 'band', axis=0)]
    ppermute x0 -> x27, starting transfers between devices: none -> 46.7 us  [permute(): return lax.ppermute(x, ('band', 'col'), pairs)]
    all_to_all x2 -> x1, blocking collectives: 34.2 us -> 11.3 us  [local(): own = lax.all_to_all(rho, 'col', split_axis=0, concat_axis=0, tiled=True)]
    ppermute x0 -> x27, waiting for transfers between devices: none -> 22.5 us  [permute(): return lax.ppermute(x, ('band', 'col'), pairs)]
    unnamed x14 -> x1, local copies, waits for them, and re-layouts: 6.6 us -> 0.01 us
    all_to_all x0 -> x1, starting transfers between devices: none -> 3.38 us  [local(): lax.all_to_all(weighted, 'band', split_axis=0, concat_axis=0, tiled=True,...]
    pallas_call x2 -> x6, Pallas kernels: 22 us -> 20.1 us  [the longest x1 13.9 us: densities(): pl.pallas_call(functools.partial(density_kernel, pairs, n_col, col_width)...]
  transfers between devices with their start and end apart: 2 -> 28, of which waited for: 2 -> 8; matrix products, arithmetic and copies ran while one was open for 0% -> 0% of each run, Pallas kernels for 0% -> 1%
where the time goes in v1:
time: 108 us; the launch traced here: 107 us
  starting transfers between devices  50.1 us (46%)
  waiting for transfers between devices  22.5 us (21%)
  Pallas kernels  20.1 us (19%)
  blocking collectives  11.3 us (10%)
  between operations  1.61 us (1%)
  local copies, waits for them, and re-layouts  1.49 us (1%)
    ppermute x27, starting transfers between devices, permute(): return lax.ppermute(x, ('band', 'col'), pairs)  46.7 us
    ppermute x27, waiting for transfers between devices, permute(): return lax.ppermute(x, ('band', 'col'), pairs)  22.5 us
    pallas_call x1, Pallas kernels, densities(): pl.pallas_call(functools.partial(density_kernel, pairs, n_col, col_width)...  13.9 us
    all_to_all x1, blocking collectives, local(): own = lax.all_to_all(rho, 'col', split_axis=0, concat_axis=0, tiled=True)  11.3 us
    pallas_call x1, Pallas kernels, product(): pl.pallas_call(functools.partial(product_kernel, [g[:2] + (len(g[2]),) fo...  4.73 us
    all_to_all x1, starting transfers between devices, local(): lax.all_to_all(weighted, 'band', split_axis=0, concat_axis=0, tiled=True,...  3.38 us
  transfers between devices with their start and end apart: 28, of which 8 were waited for; matrix products, arithmetic and copies ran while one was open for 0% of the time, Pallas kernels for 1%

profile of v1, /device:TPU:1, one launch (start us, length us, event | category | flops | bytes accessed | tf_op | source)
XLA Modules:
  0.0 107.1 jit_solution(4468058221993295368)
XLA Ops:
  1.3 1.4 %reshape.9.g_ref = s32[40,256]{1,0:T(8,128)} reshape(s32[10240]{0:T(1024)} %param.16) | data formatting | bytes 81920 | tf_op jit(solution)/shard_map/reshape | solution.py:210
  2.7 13.9 %shard_map.100 = (bf16[8,8,1280]{2,1,0:T(8,128)(2,1)}, bf16[8,8,1280]{2,1,0:T(8,128)(2,1)}) custom-call(bf16[1,64,64,128]{3,2,1,0:T(8,128)(2,1)} %v_ref.1, bf16[4,64,64,128]{3,2,1,0:T(8,128)(2,1)} %c_ref.1, bf16[432,512]{1,0:T(8,128)(2,1)} %constant.6.clone.xm_ref, bf16[64,64]{1,0:T(8,128)(2,1)} %constant.7.clone.ym_ref, ...), custom_call_target="tpu_custom_call" | custom-call | flops 2000000000 | bytes 6000000 | tf_op jit(solution)/shard_map/pallas_call | solution.py:187
  16.6 11.3 %all_to_all.10 = bf16[8,8,1280]{2,1,0:T(8,128)(2,1)S(1)} all-to-all(bf16[8,8,1280]{2,1,0:T(8,128)(2,1)} %get-tuple-element.16), channel_id=1, replica_groups=mesh['band'=32,'col'=8] {'col'}, dimensions={0} | all-to-all | bytes 327680 | tf_op jit(solution)/shard_map/all_to_all | solution.py:386
  27.9 2.1 %collective-permute-start.3 = (bf16[64,1280]{1,0:T(8,128)(2,1)S(1)}, bf16[64,1280]{1,0:T(8,128)(2,1)S(1)}, u32[]{:S(2)}, u32[]{:S(2)}) collective-permute-start(bf16[64,1280]{1,0:T(8,128)(2,1)S(1)} %bitcast.7), channel_id=1, source_target_pairs={{0,8},{1,9},{2,10},{3,11},{4,12},{5,13},{6,14},{7,15},{8,0},{9,1},... | collective-permute-start | bytes 491528 | tf_op jit(solution)/shard_map/ppermute | solution.py:363
  30.0 2.6 %collective-permute-start.12 = (bf16[64,1280]{1,0:T(8,128)(2,1)S(1)}, bf16[64,1280]{1,0:T(8,128)(2,1)S(1)}, u32[]{:S(2)}, u32[]{:S(2)}) collective-permute-start(bf16[64,1280]{1,0:T(8,128)(2,1)S(1)} %bitcast.8), channel_id=1, source_target_pairs={{0,16},{1,17},{2,18},{3,19},{4,20},{5,21},{6,22},{7,23},{8,24},{9,... | collective-permute-start | bytes 491528 | tf_op jit(solution)/shard_map/ppermute | solution.py:363
  32.6 0.0 collective-permute-done.3
  32.6 5.7 %collective-permute-start.4 = (bf16[128,1280]{1,0:T(8,128)(2,1)S(1)}, bf16[128,1280]{1,0:T(8,128)(2,1)S(1)}, u32[]{:S(2)}, u32[]{:S(2)}) collective-permute-start(bf16[128,1280]{1,0:T(8,128)(2,1)S(1)} %pad_maximum_fusion.refs_0_), channel_id=1, source_target_pairs={{0,32},{1,33},{2,34},{3,35},{4,36},{5,37},{6,38},{7,39},{8,232},{9... | collective-permute-start | bytes 983048 | tf_op jit(solution)/shard_map/ppermute | solution.py:363
  38.3 0.0 collective-permute-done.12
  38.3 0.0 collective-permute-start.13
  38.3 1.4 %collective-permute-done.13 = bf16[64,1280]{1,0:T(8,128)(2,1)S(1)} collective-permute-done((bf16[64,1280]{1,0:T(8,128)(2,1)S(1)}, bf16[64,1280]{1,0:T(8,128)(2,1)S(1)}, u32[]{:S(2)}, u32[]{:S(2)}) %collective-permute-start.13) | collective-permute-done | bytes 163872 | tf_op jit(solution)/shard_map/ppermute | solution.py:363
  39.7 5.1 %collective-permute-start.14 = (bf16[128,1280]{1,0:T(8,128)(2,1)S(1)}, bf16[128,1280]{1,0:T(8,128)(2,1)S(1)}, u32[]{:S(2)}, u32[]{:S(2)}) collective-permute-start(bf16[128,1280]{1,0:T(8,128)(2,1)S(1)} %constant_dynamic-update-slice_fusion.refs_1_), channel_id=1, source_target_pairs={{0,32},{1,33},{2,34},{3,35},{4,36},{5,37},{6,38},{7,39},{8,232},{9... | collective-permute-start | bytes 983048 | tf_op jit(solution)/shard_map/ppermute | solution.py:363
  44.8 0.0 collective-permute-done.4.refs_2_
  44.8 0.7 collective-permute-start.5
  45.5 3.4 %all-to-all-start = ((bf16[8,8,1280]{2,1,0:T(8,128)(2,1)}), bf16[8,8,1280]{2,1,0:T(8,128)(2,1)S(1)}, u32[]{:S(2)}, u32[]{:S(2)}) async-start(bf16[8,8,1280]{2,1,0:T(8,128)(2,1)} %get-tuple-element.11), calls=%async_computation | async-start | bytes 327680 | tf_op jit(solution)/shard_map/all_to_all | solution.py:383
  48.9 0.0 collective-permute-done.14.refs_3_
  48.9 3.0 %collective-permute-start.17 = (bf16[128,1280]{1,0:T(8,128)(2,1)S(1)}, bf16[128,1280]{1,0:T(8,128)(2,1)S(1)}, u32[]{:S(2)}, u32[]{:S(2)}) collective-permute-start(bf16[128,1280]{1,0:T(8,128)(2,1)S(1)} %collective-permute-done.14.refs_3_), channel_id=1, source_target_pairs={{0,32},{1,33},{2,34},{3,35},{4,36},{5,37},{6,38},{7,39},{8,232},{9... | collective-permute-start | bytes 983048 | tf_op jit(solution)/shard_map/ppermute | solution.py:363
  51.9 2.4 %collective-permute-done.5.refs_4_.refs_6_ = bf16[128,1280]{1,0:T(8,128)(2,1)S(1)} collective-permute-done((bf16[128,1280]{1,0:T(8,128)(2,1)S(1)}, bf16[128,1280]{1,0:T(8,128)(2,1)S(1)}, u32[]{:S(2)}, u32[]{:S(2)}) %collective-permute-start.5) | collective-permute-done | bytes 327712 | tf_op jit(solution)/shard_map/ppermute | solution.py:363
  54.4 3.4 %collective-permute-start.7 = (bf16[128,1280]{1,0:T(8,128)(2,1)S(1)}, bf16[128,1280]{1,0:T(8,128)(2,1)S(1)}, u32[]{:S(2)}, u32[]{:S(2)}) collective-permute-start(bf16[128,1280]{1,0:T(8,128)(2,1)S(1)} %collective-permute-done.5.refs_4_.refs_6_), channel_id=1, source_target_pairs={{0,32},{1,33},{2,34},{3,35},{4,36},{5,37},{6,38},{7,39},{8,232},{9... | collective-permute-start | bytes 983048 | tf_op jit(solution)/shard_map/ppermute | solution.py:363
  57.8 0.0 all-to-all-done
  57.8 0.1 shard_map.101
  57.9 1.4 %collective-permute-start = (bf16[64,320]{1,0:T(8,128)(2,1)S(1)}, bf16[64,320]{1,0:T(8,128)(2,1)S(1)}, u32[]{:S(2)}, u32[]{:S(2)}) collective-permute-start(bf16[64,320]{1,0:T(8,128)(2,1)S(1)} %get-tuple-element.13), channel_id=1, source_target_pairs={{0,8},{1,9},{2,10},{3,11},{4,12},{5,13},{6,14},{7,15},{8,0},{9,1},... | collective-permute-start | bytes 122888 | tf_op jit(solution)/shard_map/ppermute | solution.py:363
  59.3 2.6 %collective-permute-start.1 = (bf16[64,320]{1,0:T(8,128)(2,1)S(1)}, bf16[64,320]{1,0:T(8,128)(2,1)S(1)}, u32[]{:S(2)}, u32[]{:S(2)}) collective-permute-start(bf16[64,320]{1,0:T(8,128)(2,1)S(1)} %get-tuple-element.14), channel_id=1, source_target_pairs={{0,16},{1,17},{2,18},{3,19},{4,20},{5,21},{6,22},{7,23},{8,24},{9,... | collective-permute-start | bytes 122888 | tf_op jit(solution)/shard_map/ppermute | solution.py:363
  61.9 0.7 collective-permute-start.2
  62.5 0.0 collective-permute-done.refs_1_
  62.5 1.2 %collective-permute-done.1.refs_2_ = bf16[64,320]{1,0:T(8,128)(2,1)S(1)} collective-permute-done((bf16[64,320]{1,0:T(8,128)(2,1)S(1)}, bf16[64,320]{1,0:T(8,128)(2,1)S(1)}, u32[]{:S(2)}, u32[]{:S(2)}) %collective-permute-start.1) | collective-permute-done | bytes 40992 | tf_op jit(solution)/shard_map/ppermute | solution.py:363
  63.8 3.3 %collective-permute-done.2.refs_3_ = bf16[64,320]{1,0:T(8,128)(2,1)S(1)} collective-permute-done((bf16[64,320]{1,0:T(8,128)(2,1)S(1)}, bf16[64,320]{1,0:T(8,128)(2,1)S(1)}, u32[]{:S(2)}, u32[]{:S(2)}) %collective-permute-start.2) | collective-permute-done | bytes 40992 | tf_op jit(solution)/shard_map/ppermute | solution.py:363
  67.1 0.3 collective-permute-start.6
  67.4 0.0 collective-permute-done.17.refs_7_
  67.4 1.7 %collective-permute-start.20 = (bf16[128,1280]{1,0:T(8,128)(2,1)S(1)}, bf16[128,1280]{1,0:T(8,128)(2,1)S(1)}, u32[]{:S(2)}, u32[]{:S(2)}) collective-permute-start(bf16[128,1280]{1,0:T(8,128)(2,1)S(1)} %collective-permute-done.17.refs_7_), channel_id=1, source_target_pairs={{0,32},{1,33},{2,34},{3,35},{4,36},{5,37},{6,38},{7,39},{8,232},{9... | collective-permute-start | bytes 983048 | tf_op jit(solution)/shard_map/ppermute | solution.py:363
  69.1 4.2 %collective-permute-done.6.refs_1_ = bf16[4,64,320]{2,1,0:T(8,128)(2,1)S(1)} collective-permute-done((bf16[4,64,320]{2,1,0:T(8,128)(2,1)S(1)}, bf16[4,64,320]{2,1,0:T(8,128)(2,1)S(1)}, u32[]{:S(2)}, u32[]{:S(2)}) %collective-permute-start.6) | collective-permute-done | bytes 163872 | tf_op jit(solution)/shard_map/ppermute | solution.py:363
  73.3 0.0 collective-permute-done.7.refs_2_.refs_10_
  73.4 1.1 collective-permute-start.9
  74.4 0.7 collective-permute-start.8
  75.1 1.8 %collective-permute-start.15 = (bf16[128,1280]{1,0:T(8,128)(2,1)S(1)}, bf16[128,1280]{1,0:T(8,128)(2,1)S(1)}, u32[]{:S(2)}, u32[]{:S(2)}) collective-permute-start(bf16[128,1280]{1,0:T(8,128)(2,1)S(1)} %collective-permute-done.4.refs_2_), channel_id=1, source_target_pairs={{0,8},{1,9},{2,10},{3,11},{4,12},{5,13},{6,14},{7,15},{8,0},{9,1},... | collective-permute-start | bytes 983048 | tf_op jit(solution)/shard_map/ppermute | solution.py:363
  76.8 0.0 collective-permute-start.16
  76.9 0.0 collective-permute-done.20.refs_11_
  76.9 0.6 collective-permute-start.18
  77.5 5.6 %collective-permute-done.9.prev_ref = bf16[2,4,64,320]{3,2,1,0:T(8,128)(2,1)S(1)} collective-permute-done((bf16[2,4,64,320]{3,2,1,0:T(8,128)(2,1)S(1)}, bf16[2,4,64,320]{3,2,1,0:T(8,128)(2,1)S(1)}, u32[]{:S(2)}, u32[]{:S(2)}) %collective-permute-start.9) | collective-permute-done | bytes 327712 | tf_op jit(solution)/shard_map/ppermute | solution.py:363
  83.0 1.7 %collective-permute-start.23 = (bf16[64,1280]{1,0:T(8,128)(2,1)S(1)}, bf16[64,1280]{1,0:T(8,128)(2,1)S(1)}, u32[]{:S(2)}, u32[]{:S(2)}) collective-permute-start(bf16[64,1280]{1,0:T(8,128)(2,1)S(1)} %slice.18), channel_id=1, source_target_pairs={{0,32},{1,33},{2,34},{3,35},{4,36},{5,37},{6,38},{7,39},{8,232},{9... | collective-permute-start | bytes 491528 | tf_op jit(solution)/shard_map/ppermute | solution.py:363
  84.8 0.0 collective-permute-done.8.next_ref
  84.8 1.7 %collective-permute-start.25 = (bf16[64,1280]{1,0:T(8,128)(2,1)S(1)}, bf16[64,1280]{1,0:T(8,128)(2,1)S(1)}, u32[]{:S(2)}, u32[]{:S(2)}) collective-permute-start(bf16[64,1280]{1,0:T(8,128)(2,1)S(1)} %slice.19), channel_id=1, source_target_pairs={{0,32},{1,33},{2,34},{3,35},{4,36},{5,37},{6,38},{7,39},{8,232},{9... | collective-permute-start | bytes 491528 | tf_op jit(solution)/shard_map/ppermute | solution.py:363
  86.5 0.0 collective-permute-done.15.refs_4_
  86.5 2.9 %collective-permute-start.19 = (bf16[128,1280]{1,0:T(8,128)(2,1)S(1)}, bf16[128,1280]{1,0:T(8,128)(2,1)S(1)}, u32[]{:S(2)}, u32[]{:S(2)}) collective-permute-start(bf16[128,1280]{1,0:T(8,128)(2,1)S(1)} %collective-permute-done.17.refs_7_), channel_id=1, source_target_pairs={{0,8},{1,9},{2,10},{3,11},{4,12},{5,13},{6,14},{7,15},{8,0},{9,1},... | collective-permute-start | bytes 983048 | tf_op jit(solution)/shard_map/ppermute | solution.py:363
  89.5 0.0 collective-permute-done.16.refs_5_
  89.5 0.1 collective-permute-start.21
  89.6 0.0 collective-permute-done.18.refs_8_
  89.6 0.7 collective-permute-start.11
  90.3 0.0 collective-permute-done.23.refs_14_
  90.3 1.4 %collective-permute-start.22 = (bf16[128,1280]{1,0:T(8,128)(2,1)S(1)}, bf16[128,1280]{1,0:T(8,128)(2,1)S(1)}, u32[]{:S(2)}, u32[]{:S(2)}) collective-permute-start(bf16[128,1280]{1,0:T(8,128)(2,1)S(1)} %collective-permute-done.20.refs_11_), channel_id=1, source_target_pairs={{0,8},{1,9},{2,10},{3,11},{4,12},{5,13},{6,14},{7,15},{8,0},{9,1},... | collective-permute-start | bytes 983048 | tf_op jit(solution)/shard_map/ppermute | solution.py:363
  91.7 0.0 collective-permute-done.25.refs_16_
  91.7 0.1 collective-permute-start.10
  91.8 3.9 %collective-permute-done.11.low_ref = bf16[4,64,320]{2,1,0:T(8,128)(2,1)S(1)} collective-permute-done((bf16[4,64,320]{2,1,0:T(8,128)(2,1)S(1)}, bf16[4,64,320]{2,1,0:T(8,128)(2,1)S(1)}, u32[]{:S(2)}, u32[]{:S(2)}) %collective-permute-start.11) | collective-permute-done | bytes 163872 | tf_op jit(solution)/shard_map/ppermute | solution.py:363
  95.7 1.2 %collective-permute-start.24 = (bf16[64,1280]{1,0:T(8,128)(2,1)S(1)}, bf16[64,1280]{1,0:T(8,128)(2,1)S(1)}, u32[]{:S(2)}, u32[]{:S(2)}) collective-permute-start(bf16[64,1280]{1,0:T(8,128)(2,1)S(1)} %collective-permute-done.23.refs_14_), channel_id=1, source_target_pairs={{0,8},{1,9},{2,10},{3,11},{4,12},{5,13},{6,14},{7,15},{8,0},{9,1},... | collective-permute-start | bytes 491528 | tf_op jit(solution)/shard_map/ppermute | solution.py:363
  96.9 0.5 collective-permute-done.10.high_ref
  97.4 3.5 %collective-permute-start.26 = (bf16[64,1280]{1,0:T(8,128)(2,1)S(1)}, bf16[64,1280]{1,0:T(8,128)(2,1)S(1)}, u32[]{:S(2)}, u32[]{:S(2)}) collective-permute-start(bf16[64,1280]{1,0:T(8,128)(2,1)S(1)} %collective-permute-done.25.refs_16_), channel_id=1, source_target_pairs={{0,8},{1,9},{2,10},{3,11},{4,12},{5,13},{6,14},{7,15},{8,0},{9,1},... | collective-permute-start | bytes 491528 | tf_op jit(solution)/shard_map/ppermute | solution.py:363
  100.9 1.3 %shard_map.104.l_ref = bf16[640,2048]{1,0:T(8,128)(2,1)S(1)} custom-call(bf16[2,4,64,320]{3,2,1,0:T(8,128)(2,1)S(1)} %shard_map.103.own_ref, bf16[2,4,64,320]{3,2,1,0:T(8,128)(2,1)S(1)} %collective-permute-done.8.next_ref, bf16[2,4,64,320]{3,2,1,0:T(8,128)(2,1)S(1)} %collective-permute-done.9.prev_ref, ...), custom_call_target="tpu_custom_call" | custom-call | tf_op jit(solution)/shard_map/pallas_call | solution.py:285
  102.2 0.0 collective-permute-done.19.refs_9_
  102.2 0.0 collective-permute-done.24.refs_15_
  102.2 0.0 collective-permute-done.21.refs_12_
  102.2 0.0 collective-permute-done.22.refs_13_
  102.2 0.0 collective-permute-done.26.refs_17_
  102.2 4.7 %shard_map.105 = f32[2,320,1280]{2,1,0:T(8,128)} custom-call(bf16[640,2048]{1,0:T(8,128)(2,1)S(1)} %shard_map.104.l_ref, bf16[128,1280]{1,0:T(8,128)(2,1)S(1)} %pad_maximum_fusion.refs_0_, bf16[128,1280]{1,0:T(8,128)(2,1)S(1)} %constant_dynamic-update-slice_fusion.refs_1_, bf16[128,1280]{1,0:T(8,128)(2,1)S(1)} %collective-permute-done.4.refs_2_, ...), custom_call_target="tpu_custom_call" | custom-call | tf_op jit(solution)/shard_map/pallas_call | solution.py:344
  (9 shorter events, 0.2 us)
Async XLA Ops:
  27.9 4.7 %collective-permute-start.3 = (bf16[64,1280]{1,0:T(8,128)(2,1)S(1)}, bf16[64,1280]{1,0:T(8,128)(2,1)S(1)}, u32[]{:S(2)}, u32[]{:S(2)}) collective-permute-start(bf16[64,1280]{1,0:T(8,128)(2,1)S(1)} %bitcast.7), channel_id=1, source_target_pairs={{0,8},{1,9},{2,10},{3,11},{4,12},{5,13},{6,14},{7,15},{8,0},{9,1},... | collective-permute-start | bytes 491528 | tf_op jit(solution)/shard_map/ppermute | solution.py:363
  30.0 8.3 %collective-permute-start.12 = (bf16[64,1280]{1,0:T(8,128)(2,1)S(1)}, bf16[64,1280]{1,0:T(8,128)(2,1)S(1)}, u32[]{:S(2)}, u32[]{:S(2)}) collective-permute-start(bf16[64,1280]{1,0:T(8,128)(2,1)S(1)} %bitcast.8), channel_id=1, source_target_pairs={{0,16},{1,17},{2,18},{3,19},{4,20},{5,21},{6,22},{7,23},{8,24},{9,... | collective-permute-start | bytes 491528 | tf_op jit(solution)/shard_map/ppermute | solution.py:363
  32.6 12.2 %collective-permute-start.4 = (bf16[128,1280]{1,0:T(8,128)(2,1)S(1)}, bf16[128,1280]{1,0:T(8,128)(2,1)S(1)}, u32[]{:S(2)}, u32[]{:S(2)}) collective-permute-start(bf16[128,1280]{1,0:T(8,128)(2,1)S(1)} %pad_maximum_fusion.refs_0_), channel_id=1, source_target_pairs={{0,32},{1,33},{2,34},{3,35},{4,36},{5,37},{6,38},{7,39},{8,232},{9... | collective-permute-start | bytes 983048 | tf_op jit(solution)/shard_map/ppermute | solution.py:363
  38.3 1.4 %collective-permute-start.13 = (bf16[64,1280]{1,0:T(8,128)(2,1)S(1)}, bf16[64,1280]{1,0:T(8,128)(2,1)S(1)}, u32[]{:S(2)}, u32[]{:S(2)}) collective-permute-start(bf16[64,1280]{1,0:T(8,128)(2,1)S(1)} %collective-permute-done.12), channel_id=1, source_target_pairs={{0,8},{1,9},{2,10},{3,11},{4,12},{5,13},{6,14},{7,15},{8,0},{9,1},... | collective-permute-start | bytes 491528 | tf_op jit(solution)/shard_map/ppermute | solution.py:363
  39.7 9.2 %collective-permute-start.14 = (bf16[128,1280]{1,0:T(8,128)(2,1)S(1)}, bf16[128,1280]{1,0:T(8,128)(2,1)S(1)}, u32[]{:S(2)}, u32[]{:S(2)}) collective-permute-start(bf16[128,1280]{1,0:T(8,128)(2,1)S(1)} %constant_dynamic-update-slice_fusion.refs_1_), channel_id=1, source_target_pairs={{0,32},{1,33},{2,34},{3,35},{4,36},{5,37},{6,38},{7,39},{8,232},{9... | collective-permute-start | bytes 983048 | tf_op jit(solution)/shard_map/ppermute | solution.py:363
  44.8 9.6 %collective-permute-start.5 = (bf16[128,1280]{1,0:T(8,128)(2,1)S(1)}, bf16[128,1280]{1,0:T(8,128)(2,1)S(1)}, u32[]{:S(2)}, u32[]{:S(2)}) collective-permute-start(bf16[128,1280]{1,0:T(8,128)(2,1)S(1)} %collective-permute-done.4.refs_2_), channel_id=1, source_target_pairs={{0,32},{1,33},{2,34},{3,35},{4,36},{5,37},{6,38},{7,39},{8,232},{9... | collective-permute-start | bytes 983048 | tf_op jit(solution)/shard_map/ppermute | solution.py:363
  45.5 12.3 %all-to-all-start = ((bf16[8,8,1280]{2,1,0:T(8,128)(2,1)}), bf16[8,8,1280]{2,1,0:T(8,128)(2,1)S(1)}, u32[]{:S(2)}, u32[]{:S(2)}) async-start(bf16[8,8,1280]{2,1,0:T(8,128)(2,1)} %get-tuple-element.11), calls=%async_computation | async-start | bytes 327680 | tf_op jit(solution)/shard_map/all_to_all | solution.py:383
  48.9 18.5 %collective-permute-start.17 = (bf16[128,1280]{1,0:T(8,128)(2,1)S(1)}, bf16[128,1280]{1,0:T(8,128)(2,1)S(1)}, u32[]{:S(2)}, u32[]{:S(2)}) collective-permute-start(bf16[128,1280]{1,0:T(8,128)(2,1)S(1)} %collective-permute-done.14.refs_3_), channel_id=1, source_target_pairs={{0,32},{1,33},{2,34},{3,35},{4,36},{5,37},{6,38},{7,39},{8,232},{9... | collective-permute-start | bytes 983048 | tf_op jit(solution)/shard_map/ppermute | solution.py:363
  54.4 19.0 %collective-permute-start.7 = (bf16[128,1280]{1,0:T(8,128)(2,1)S(1)}, bf16[128,1280]{1,0:T(8,128)(2,1)S(1)}, u32[]{:S(2)}, u32[]{:S(2)}) collective-permute-start(bf16[128,1280]{1,0:T(8,128)(2,1)S(1)} %collective-permute-done.5.refs_4_.refs_6_), channel_id=1, source_target_pairs={{0,32},{1,33},{2,34},{3,35},{4,36},{5,37},{6,38},{7,39},{8,232},{9... | collective-permute-start | bytes 983048 | tf_op jit(solution)/shard_map/ppermute | solution.py:363
  57.9 4.6 %collective-permute-start = (bf16[64,320]{1,0:T(8,128)(2,1)S(1)}, bf16[64,320]{1,0:T(8,128)(2,1)S(1)}, u32[]{:S(2)}, u32[]{:S(2)}) collective-permute-start(bf16[64,320]{1,0:T(8,128)(2,1)S(1)} %get-tuple-element.13), channel_id=1, source_target_pairs={{0,8},{1,9},{2,10},{3,11},{4,12},{5,13},{6,14},{7,15},{8,0},{9,1},... | collective-permute-start | bytes 122888 | tf_op jit(solution)/shard_map/ppermute | solution.py:363
  59.3 4.5 %collective-permute-start.1 = (bf16[64,320]{1,0:T(8,128)(2,1)S(1)}, bf16[64,320]{1,0:T(8,128)(2,1)S(1)}, u32[]{:S(2)}, u32[]{:S(2)}) collective-permute-start(bf16[64,320]{1,0:T(8,128)(2,1)S(1)} %get-tuple-element.14), channel_id=1, source_target_pairs={{0,16},{1,17},{2,18},{3,19},{4,20},{5,21},{6,22},{7,23},{8,24},{9,... | collective-permute-start | bytes 122888 | tf_op jit(solution)/shard_map/ppermute | solution.py:363
  61.9 5.2 %collective-permute-start.2 = (bf16[64,320]{1,0:T(8,128)(2,1)S(1)}, bf16[64,320]{1,0:T(8,128)(2,1)S(1)}, u32[]{:S(2)}, u32[]{:S(2)}) collective-permute-start(bf16[64,320]{1,0:T(8,128)(2,1)S(1)} %get-tuple-element.15), channel_id=1, source_target_pairs={{0,24},{1,25},{2,26},{3,27},{4,28},{5,29},{6,30},{7,31},{8,16},{9,... | collective-permute-start | bytes 122888 | tf_op jit(solution)/shard_map/ppermute | solution.py:363
  67.1 6.2 %collective-permute-start.6 = (bf16[4,64,320]{2,1,0:T(8,128)(2,1)S(1)}, bf16[4,64,320]{2,1,0:T(8,128)(2,1)S(1)}, u32[]{:S(2)}, u32[]{:S(2)}) collective-permute-start(bf16[4,64,320]{2,1,0:T(8,128)(2,1)S(1)} %shard_map.102.refs_0_), channel_id=1, source_target_pairs={{0,1},{1,0},{2,3},{3,2},{4,5},{5,4},{6,7},{7,6},{8,9},{9,8},{10,11... | collective-permute-start | bytes 491528 | tf_op jit(solution)/shard_map/ppermute | solution.py:363
  67.4 9.5 %collective-permute-start.20 = (bf16[128,1280]{1,0:T(8,128)(2,1)S(1)}, bf16[128,1280]{1,0:T(8,128)(2,1)S(1)}, u32[]{:S(2)}, u32[]{:S(2)}) collective-permute-start(bf16[128,1280]{1,0:T(8,128)(2,1)S(1)} %collective-permute-done.17.refs_7_), channel_id=1, source_target_pairs={{0,32},{1,33},{2,34},{3,35},{4,36},{5,37},{6,38},{7,39},{8,232},{9... | collective-permute-start | bytes 983048 | tf_op jit(solution)/shard_map/ppermute | solution.py:363
  73.4 9.7 %collective-permute-start.9 = (bf16[2,4,64,320]{3,2,1,0:T(8,128)(2,1)S(1)}, bf16[2,4,64,320]{3,2,1,0:T(8,128)(2,1)S(1)}, u32[]{:S(2)}, u32[]{:S(2)}) collective-permute-start(bf16[2,4,64,320]{3,2,1,0:T(8,128)(2,1)S(1)} %shard_map.103.own_ref), channel_id=1, source_target_pairs={{0,6},{1,7},{2,0},{3,1},{4,2},{5,3},{6,4},{7,5},{8,14},{9,15},{10,... | collective-permute-start | bytes 983048 | tf_op jit(solution)/shard_map/ppermute | solution.py:363
  74.4 10.4 %collective-permute-start.8 = (bf16[2,4,64,320]{3,2,1,0:T(8,128)(2,1)S(1)}, bf16[2,4,64,320]{3,2,1,0:T(8,128)(2,1)S(1)}, u32[]{:S(2)}, u32[]{:S(2)}) collective-permute-start(bf16[2,4,64,320]{3,2,1,0:T(8,128)(2,1)S(1)} %shard_map.103.own_ref), channel_id=1, source_target_pairs={{0,2},{1,3},{2,4},{3,5},{4,6},{5,7},{6,0},{7,1},{8,10},{9,11},{10,... | collective-permute-start | bytes 983048 | tf_op jit(solution)/shard_map/ppermute | solution.py:363
  75.1 11.4 %collective-permute-start.15 = (bf16[128,1280]{1,0:T(8,128)(2,1)S(1)}, bf16[128,1280]{1,0:T(8,128)(2,1)S(1)}, u32[]{:S(2)}, u32[]{:S(2)}) collective-permute-start(bf16[128,1280]{1,0:T(8,128)(2,1)S(1)} %collective-permute-done.4.refs_2_), channel_id=1, source_target_pairs={{0,8},{1,9},{2,10},{3,11},{4,12},{5,13},{6,14},{7,15},{8,0},{9,1},... | collective-permute-start | bytes 983048 | tf_op jit(solution)/shard_map/ppermute | solution.py:363
  76.8 12.6 %collective-permute-start.16 = (bf16[128,1280]{1,0:T(8,128)(2,1)S(1)}, bf16[128,1280]{1,0:T(8,128)(2,1)S(1)}, u32[]{:S(2)}, u32[]{:S(2)}) collective-permute-start(bf16[128,1280]{1,0:T(8,128)(2,1)S(1)} %collective-permute-done.14.refs_3_), channel_id=1, source_target_pairs={{0,8},{1,9},{2,10},{3,11},{4,12},{5,13},{6,14},{7,15},{8,0},{9,1},... | collective-permute-start | bytes 983048 | tf_op jit(solution)/shard_map/ppermute | solution.py:363
  76.9 12.7 %collective-permute-start.18 = (bf16[128,1280]{1,0:T(8,128)(2,1)S(1)}, bf16[128,1280]{1,0:T(8,128)(2,1)S(1)}, u32[]{:S(2)}, u32[]{:S(2)}) collective-permute-start(bf16[128,1280]{1,0:T(8,128)(2,1)S(1)} %collective-permute-done.5.refs_4_.refs_6_), channel_id=1, source_target_pairs={{0,8},{1,9},{2,10},{3,11},{4,12},{5,13},{6,14},{7,15},{8,0},{9,1},... | collective-permute-start | bytes 983048 | tf_op jit(solution)/shard_map/ppermute | solution.py:363
  83.0 7.3 %collective-permute-start.23 = (bf16[64,1280]{1,0:T(8,128)(2,1)S(1)}, bf16[64,1280]{1,0:T(8,128)(2,1)S(1)}, u32[]{:S(2)}, u32[]{:S(2)}) collective-permute-start(bf16[64,1280]{1,0:T(8,128)(2,1)S(1)} %slice.18), channel_id=1, source_target_pairs={{0,32},{1,33},{2,34},{3,35},{4,36},{5,37},{6,38},{7,39},{8,232},{9... | collective-permute-start | bytes 491528 | tf_op jit(solution)/shard_map/ppermute | solution.py:363
  84.8 6.9 %collective-permute-start.25 = (bf16[64,1280]{1,0:T(8,128)(2,1)S(1)}, bf16[64,1280]{1,0:T(8,128)(2,1)S(1)}, u32[]{:S(2)}, u32[]{:S(2)}) collective-permute-start(bf16[64,1280]{1,0:T(8,128)(2,1)S(1)} %slice.19), channel_id=1, source_target_pairs={{0,32},{1,33},{2,34},{3,35},{4,36},{5,37},{6,38},{7,39},{8,232},{9... | collective-permute-start | bytes 491528 | tf_op jit(solution)/shard_map/ppermute | solution.py:363
  86.5 15.6 %collective-permute-start.19 = (bf16[128,1280]{1,0:T(8,128)(2,1)S(1)}, bf16[128,1280]{1,0:T(8,128)(2,1)S(1)}, u32[]{:S(2)}, u32[]{:S(2)}) collective-permute-start(bf16[128,1280]{1,0:T(8,128)(2,1)S(1)} %collective-permute-done.17.refs_7_), channel_id=1, source_target_pairs={{0,8},{1,9},{2,10},{3,11},{4,12},{5,13},{6,14},{7,15},{8,0},{9,1},... | collective-permute-start | bytes 983048 | tf_op jit(solution)/shard_map/ppermute | solution.py:363
  89.5 12.7 %collective-permute-start.21 = (bf16[128,1280]{1,0:T(8,128)(2,1)S(1)}, bf16[128,1280]{1,0:T(8,128)(2,1)S(1)}, u32[]{:S(2)}, u32[]{:S(2)}) collective-permute-start(bf16[128,1280]{1,0:T(8,128)(2,1)S(1)} %collective-permute-done.7.refs_2_.refs_10_), channel_id=1, source_target_pairs={{0,8},{1,9},{2,10},{3,11},{4,12},{5,13},{6,14},{7,15},{8,0},{9,1},... | collective-permute-start | bytes 983048 | tf_op jit(solution)/shard_map/ppermute | solution.py:363
  89.6 6.1 %collective-permute-start.11 = (bf16[4,64,320]{2,1,0:T(8,128)(2,1)S(1)}, bf16[4,64,320]{2,1,0:T(8,128)(2,1)S(1)}, u32[]{:S(2)}, u32[]{:S(2)}) collective-permute-start(bf16[4,64,320]{2,1,0:T(8,128)(2,1)S(1)} %slice_bitcast_fusion), channel_id=1, source_target_pairs={{0,6},{1,7},{2,0},{3,1},{4,2},{5,3},{6,4},{7,5},{8,14},{9,15},{10,... | collective-permute-start | bytes 491528 | tf_op jit(solution)/shard_map/ppermute | solution.py:363
  90.3 11.9 %collective-permute-start.22 = (bf16[128,1280]{1,0:T(8,128)(2,1)S(1)}, bf16[128,1280]{1,0:T(8,128)(2,1)S(1)}, u32[]{:S(2)}, u32[]{:S(2)}) collective-permute-start(bf16[128,1280]{1,0:T(8,128)(2,1)S(1)} %collective-permute-done.20.refs_11_), channel_id=1, source_target_pairs={{0,8},{1,9},{2,10},{3,11},{4,12},{5,13},{6,14},{7,15},{8,0},{9,1},... | collective-permute-start | bytes 983048 | tf_op jit(solution)/shard_map/ppermute | solution.py:363
  91.7 5.7 %collective-permute-start.10 = (bf16[4,64,320]{2,1,0:T(8,128)(2,1)S(1)}, bf16[4,64,320]{2,1,0:T(8,128)(2,1)S(1)}, u32[]{:S(2)}, u32[]{:S(2)}) collective-permute-start(bf16[4,64,320]{2,1,0:T(8,128)(2,1)S(1)} %slice_bitcast_fusion.1), channel_id=1, source_target_pairs={{0,2},{1,3},{2,4},{3,5},{4,6},{5,7},{6,0},{7,1},{8,10},{9,11},{10,... | collective-permute-start | bytes 491528 | tf_op jit(solution)/shard_map/ppermute | solution.py:363
  95.7 6.5 %collective-permute-start.24 = (bf16[64,1280]{1,0:T(8,128)(2,1)S(1)}, bf16[64,1280]{1,0:T(8,128)(2,1)S(1)}, u32[]{:S(2)}, u32[]{:S(2)}) collective-permute-start(bf16[64,1280]{1,0:T(8,128)(2,1)S(1)} %collective-permute-done.23.refs_14_), channel_id=1, source_target_pairs={{0,8},{1,9},{2,10},{3,11},{4,12},{5,13},{6,14},{7,15},{8,0},{9,1},... | collective-permute-start | bytes 491528 | tf_op jit(solution)/shard_map/ppermute | solution.py:363
  97.4 4.8 %collective-permute-start.26 = (bf16[64,1280]{1,0:T(8,128)(2,1)S(1)}, bf16[64,1280]{1,0:T(8,128)(2,1)S(1)}, u32[]{:S(2)}, u32[]{:S(2)}) collective-permute-start(bf16[64,1280]{1,0:T(8,128)(2,1)S(1)} %collective-permute-done.25.refs_16_), channel_id=1, source_target_pairs={{0,8},{1,9},{2,10},{3,11},{4,12},{5,13},{6,14},{7,15},{8,0},{9,1},... | collective-permute-start | bytes 491528 | tf_op jit(solution)/shard_map/ppermute | solution.py:363

commit v2 on v1

--- a/solution.py
+++ b/solution.py
@@ -14,8 +14,8 @@
 NPW = 10240
 QUAD = 4
 TILE = 256
-VMEM_LIMIT = 60 * 1024 * 1024
-SMALL_LIMIT = 16 * 1024 * 1024
+VMEM_LIMIT = 56 * 1024 * 1024
+SMALL_LIMIT = 8 * 1024 * 1024
 
 
 def sphere_radius():
@@ -82,10 +82,14 @@
     return ((index + NG // 2) & (NG - 1)) - NG // 2
 
 
+def wide_row(ref, which):
+    return jnp.concatenate([ref[pl.ds(2 * which, 1), :], ref[pl.ds(2 * which + 1, 1), :]], axis=1)
+
+
 def density_kernel(
     pairs, dests, col_width,
     v_ref, c_ref, xm_ref, ym_ref, zm_ref, g_ref, ev_ref, ec_ref, ov_ref, oc_ref,
-    rho_ref, weighted_ref,
+    rho_ref, row_ref,
     first_ref, second_ref, pos_ref, kz_ref, flat_ref,
 ):
     step = pl.program_id(0)
@@ -147,15 +151,16 @@
         def body(dest, carry):
             for k in range(blocks):
                 which = dest * blocks + k
-                pos = pos_ref[pl.ds(which, 1), :]
-                kz = kz_ref[pl.ds(which, 1), :]
+                pos = wide_row(pos_ref, which)
+                kz = wide_row(kz_ref, which)
                 pick = jnp.where(row_id == pos, 1.0, 0.0).astype(jnp.bfloat16)
                 found = jnp.dot(third, pick, preferred_element_type=jnp.float32)
                 found = found.reshape(NK, 2 * pairs, 256)
                 acc = jnp.zeros((2 * pairs, 256), jnp.float32)
                 for i in range(NK):
                     acc = jnp.where(kz == i, found[i], acc)
-                rho_ref[dest, :, k * 256 : (k + 1) * 256] = acc.astype(jnp.bfloat16)
+                for copy in range(2):
+                    rho_ref[copy, dest, :, k * 256 : (k + 1) * 256] = acc.astype(jnp.bfloat16)
                 flat_ref[which] = acc
             return carry
 
@@ -168,10 +173,13 @@
             energy = jnp.where(which_pair == p, ev_ref[0] - ec_ref[p], energy)
         weight = (occ_diff / energy / math.sqrt(1024))[:, :1]
 
+        width = col_width // QUAD
+
         def weigh(dest, carry):
-            for k in range(blocks):
-                wide = flat_ref[dest * blocks + k] * weight
-                weighted_ref[dest, :, k * 256 : (k + 1) * 256] = wide.astype(jnp.bfloat16)
+            wide = jnp.concatenate([flat_ref[dest * blocks + k] for k in range(blocks)], axis=1)
+            wide = (wide * weight).astype(jnp.bfloat16).astype(jnp.float32)
+            for k in range(QUAD):
+                row_ref[dest * QUAD + k] = wide[:, k * width : (k + 1) * width].astype(jnp.bfloat16)
             return carry
 
         lax.fori_loop(0, dests, weigh, 0)
@@ -191,88 +199,81 @@
             pl.BlockSpec((1, NG, 16, 2 * NG), lambda s: (0, 0, s, 0)),
             pl.BlockSpec((pairs, NG, 16, 2 * NG), lambda s: (0, 0, s, 0)),
             whole(xm.shape), whole(ym.shape), whole(zm.shape),
-            whole((NPW // 256, 256)),
+            whole((NPW // 128, 128)),
             smem, smem, smem, smem,
         ],
-        out_specs=[whole((n_col, 2 * pairs, col_width))] * 2,
-        out_shape=[jax.ShapeDtypeStruct((n_col, 2 * pairs, col_width), jnp.bfloat16)] * 2,
+        out_specs=[
+            whole((2, n_col, 2 * pairs, col_width)),
+            whole((n_col * QUAD, 2 * pairs, col_width // QUAD)),
+        ],
+        out_shape=[
+            jax.ShapeDtypeStruct((2, n_col, 2 * pairs, col_width), jnp.bfloat16),
+            jax.ShapeDtypeStruct((n_col * QUAD, 2 * pairs, col_width // QUAD), jnp.bfloat16),
+        ],
         scratch_shapes=[
             pltpu.VMEM((NK, NG, lanes), jnp.bfloat16),
             pltpu.VMEM((ROWS, lanes), jnp.float32),
-            pltpu.VMEM((NPW // 256, 256), jnp.int32),
-            pltpu.VMEM((NPW // 256, 256), jnp.int32),
+            pltpu.VMEM((NPW // 128, 128), jnp.int32),
+            pltpu.VMEM((NPW // 128, 128), jnp.int32),
             pltpu.VMEM((NPW // 256, 2 * pairs, 256), jnp.float32),
         ],
         compiler_params=pltpu.CompilerParams(vmem_limit_bytes=VMEM_LIMIT),
         cost_estimate=pl.CostEstimate(flops=2 * 10**9, bytes_accessed=6 * 10**6, transcendentals=0),
     )(
         valence, conduction, jnp.asarray(xm), jnp.asarray(ym), jnp.asarray(zm),
-        gvec_index.reshape(NPW // 256, 256),
+        gvec_index.reshape(NPW // 128, 128),
         energy_valence, energy_conduction, occ_valence, occ_conduction,
     )
 
 
-def split_kernel(x_ref, out0_ref, out1_ref, out2_ref, out3_ref, hold_ref):
-    me = lax.axis_index("band") % QUAD
-    width = out0_ref.shape[-1]
-    for k in range(QUAD):
-        hold_ref[k] = x_ref[:, k * width : (k + 1) * width]
-    for k, ref in enumerate((out0_ref, out1_ref, out2_ref, out3_ref)):
-        ref[...] = hold_ref[me ^ k]
-
-
-def split(x):
-    rows, total = x.shape
-    return pl.pallas_call(
-        split_kernel,
-        out_shape=[jax.ShapeDtypeStruct((rows, total // QUAD), jnp.bfloat16)] * QUAD,
-        scratch_shapes=[pltpu.VMEM((QUAD, rows, total // QUAD), jnp.bfloat16)],
-        compiler_params=pltpu.CompilerParams(vmem_limit_bytes=SMALL_LIMIT),
-    )(x)
-
-
-def stack_kernel(*refs):
-    for k, ref in enumerate(refs[:-2]):
-        refs[-1][k] = ref[...]
-
-
-def stack(parts, after):
+def spread_kernel(in_ref, after_ref, out_ref):
+    core = lax.axis_index("band") % 2
+    for j in range(out_ref.shape[1]):
+        both = jnp.concatenate(
+            [
+                in_ref[2 * j + core].astype(jnp.float32),
+                in_ref[2 * j + 1 - core].astype(jnp.float32),
+            ],
+            axis=1,
+        ).astype(jnp.bfloat16)
+        for dest in range(out_ref.shape[0]):
+            out_ref[dest, j] = both
+
+
+def spread(x, copies, after):
+    n_band, po, width = x.shape
     vmem = pl.BlockSpec(memory_space=pltpu.VMEM)
     return pl.pallas_call(
-        stack_kernel,
-        in_specs=[vmem] * len(parts) + [pl.BlockSpec(memory_space=pl.ANY)],
+        spread_kernel,
+        in_specs=[vmem, pl.BlockSpec(memory_space=pl.ANY)],
         out_specs=vmem,
-        out_shape=jax.ShapeDtypeStruct((len(parts),) + parts[0].shape, jnp.bfloat16),
+        out_shape=jax.ShapeDtypeStruct((copies, n_band // 2, po, 2 * width), jnp.bfloat16),
         compiler_params=pltpu.CompilerParams(vmem_limit_bytes=SMALL_LIMIT),
-    )(*parts, after)
-
-
-def left_kernel(n_col, depth, own_ref, next_ref, prev_ref, high_ref, low_ref, out_ref, hold_ref):
-    col = lax.axis_index("col")
-    plane = lax.axis_index("band") // QUAD
-    xs = n_col // 2
-    x, y = col // 2, col % 2
-
-    def put(source, ref):
-        hold_ref[source] = ref[...].astype(jnp.float32)
-
-    for k in range(2):
-        put(x * 2 + (y ^ k), own_ref.at[k])
-        put((x + xs - 1) % xs * 2 + (y ^ k), next_ref.at[k])
-        put((x + 1) % xs * 2 + (y ^ k), prev_ref.at[k])
-    put((x + 2) % xs * 2 + y, high_ref)
-    put((x + 2) % xs * 2 + (y ^ 1), low_ref)
-    n, quad, rows, width = hold_ref.shape
-    po = rows // depth
+        cost_estimate=pl.CostEstimate(flops=1000, bytes_accessed=1000, transcendentals=0),
+    )(x, after)
+
+
+def left_kernel(in_ref, out_ref, hold_ref):
+    band = lax.axis_index("band")
+    plane = band // QUAD
+    n, blocks, po, double = hold_ref.shape
+    duo = 2
+    depth = blocks // duo
+    width = double // 2
+    for v in range(n):
+        hold_ref[v] = in_ref[v].astype(jnp.float32)
     turns = [0]
     for step in range(1, depth // 2):
         turns += [step, depth - step]
     turns.append(depth // 2)
-    depth_rows = quad * n * po
+    depth_rows = 2 * duo * n * po
     for slot, turn in enumerate(turns):
-        source = pl.multiple_of((plane + depth - turn) % depth * po, po)
-        f = hold_ref[:, :, pl.ds(source, po), :]
-        f = jnp.concatenate([f[:, k] for k in range(quad)], axis=0)
+        source = (plane + depth - turn) % depth
+        parts = []
+        for high in range(duo):
+            f = hold_ref[:, source * duo + high]
+            parts += [f[:, :, :width], f[:, :, width:]]
+        f = jnp.concatenate(parts, axis=0)
         swapped = jnp.concatenate([f[:, po // 2 :], -f[:, : po // 2]], axis=1)
         for which, src in enumerate((f, swapped)):
             out_ref[which * width : (which + 1) * width, slot * depth_rows : (slot + 1) * depth_rows] = (
@@ -280,14 +281,15 @@
             )
 
 
-def left(n_col, depth, parts):
-    _, quad, rows, width = parts[0].shape
+def left(rows):
+    n, blocks, po, double = rows.shape
     return pl.pallas_call(
-        functools.partial(left_kernel, n_col, depth),
-        out_shape=jax.ShapeDtypeStruct((2 * width, depth * quad * rows), jnp.bfloat16),
-        scratch_shapes=[pltpu.VMEM((n_col, quad, rows, width), jnp.float32)],
+        left_kernel,
+        out_shape=jax.ShapeDtypeStruct((double, blocks * 2 * n * po), jnp.bfloat16),
+        scratch_shapes=[pltpu.VMEM(rows.shape, jnp.float32)],
         compiler_params=pltpu.CompilerParams(vmem_limit_bytes=SMALL_LIMIT),
-    )(*parts)
+        cost_estimate=pl.CostEstimate(flops=1000, bytes_accessed=1000, transcendentals=0),
+    )(rows)
 
 
 def product_on(core, turns, l_ref, blocks, out_ref, out_buf, sem):
@@ -351,6 +353,7 @@
             pltpu.SemaphoreType.DMA((total // TILE,)),
         ],
         compiler_params=pltpu.CompilerParams(vmem_limit_bytes=SMALL_LIMIT),
+        cost_estimate=pl.CostEstimate(flops=1000, bytes_accessed=1000, transcendentals=0),
     )(lhs, *blocks)
 
 
@@ -368,51 +371,44 @@
 ):
     n_col, n_band = lax.axis_size("col"), lax.axis_size("band")
     depth = n_band // QUAD
-    xs = n_col // 2
     send = functools.partial(permute, n_band=n_band, n_col=n_col)
     shift = lambda band, by: (band // QUAD + by) % depth * QUAD + band % QUAD
     ring = lambda x: send(x, move=lambda b, c: (shift(b, 1 if b % 2 == 0 else -1), c))
     swap = lambda x: send(x, move=lambda b, c: (b ^ 1, c))
-    high = lambda x: send(x, move=lambda b, c: (b ^ 2, c))
-    along_x = lambda x, by: send(x, move=lambda b, c: (b, (c // 2 + by) % xs * 2 + c % 2))
     rho, weighted = densities(
         valence, conduction, energy_valence, energy_conduction, occ_valence, occ_conduction,
         gvec_index, n_col,
     )
-    lines = [[z * QUAD + q for z in range(depth)] for q in range(QUAD)]
-    weighted = lax.all_to_all(
-        weighted, "band", split_axis=0, concat_axis=0, tiled=True, axis_index_groups=lines
+    sheets = [
+        [(z * QUAD + high * 2 + core) * n_col + c for high in range(2) for c in range(n_col)]
+        for z in range(depth)
+        for core in range(2)
+    ]
+    rho = rho.reshape((2 * n_col,) + rho.shape[2:])
+    own = lax.all_to_all(
+        rho, ("band", "col"), split_axis=0, concat_axis=0, tiled=True, axis_index_groups=sheets
     )
-    own = lax.all_to_all(rho, "col", split_axis=0, concat_axis=0, tiled=True)
-    size = own.shape[0] * own.shape[1]
-    own = own.reshape(size, own.shape[2])
-    weighted = weighted.reshape(size, weighted.shape[2])
-
-    across = high(own)
-    near_ring = [jnp.concatenate([own, swap(own)], axis=0)]
+    size = n_col * own.shape[1]
+    own = own.reshape(2 * size, own.shape[2])
+    sibling = swap(own)
+    near_ring = [jnp.concatenate([own[:size], sibling[:size]], axis=0)]
     near_ring.append(ring(near_ring[0]))
-    parts = split(weighted)
-    parts = [parts[0]] + [
-        send(parts[k], move=lambda b, c, k=k: (b ^ k, c)) for k in range(1, QUAD)
-    ]
-    far_ring = [jnp.concatenate([across, swap(across)], axis=0)]
+    far_ring = [jnp.concatenate([own[size:], sibling[size:]], axis=0)]
     far_ring.append(ring(far_ring[0]))
+    rows = lax.all_to_all(weighted, "band", split_axis=0, concat_axis=0, tiled=True)
     near_ring.append(ring(near_ring[1]))
-    mine = stack(parts, near_ring[2])
-    beside = send(mine, move=lambda b, c: (b, c ^ 1))
     far_ring.append(ring(far_ring[1]))
+    rows = spread(rows, n_col, near_ring[2])
+    rows = lax.all_to_all(rows, "col", split_axis=0, concat_axis=0, tiled=True)
     near_ring.append(ring(near_ring[2]))
-    pair = stack([mine, beside], near_ring[3])
-    after, before = along_x(pair, 1), along_x(pair, -1)
     far_ring.append(ring(far_ring[2]))
     last = [ring(near_ring[-1][:size]), ring(far_ring[-1][:size])]
-    parts = [pair, after, before, along_x(after[0], 1), along_x(before[1], -1)]
     groups = [(0, 0, (near_ring[0], far_ring[0]))]
     for step in range(1, depth // 2):
         groups.append((step, 0, (near_ring[step], far_ring[step])))
         groups.append((step, 1, (swap(near_ring[step]), swap(far_ring[step]))))
     groups.append((depth // 2, 0, (last[0], swap(last[0]), last[1], swap(last[1]))))
-    return product(left(n_col, depth, parts), groups)
+    return product(left(rows), groups)
 
 
 def solution(mesh):

time: 108 us -> 97.9 us (0.906)
  starting transfers between devices: 50.1 us -> 38.3 us
  waiting for transfers between devices: 22.5 us -> 16.1 us
  blocking collectives: 11.3 us -> 15.5 us
  Pallas kernels: 20.1 us -> 23.7 us
    ppermute x27 -> x17, starting transfers between devices: 46.7 us -> 29.4 us  [permute(): return lax.ppermute(x, ('band', 'col'), pairs)]
    ppermute x27 -> x17, waiting for transfers between devices: 22.5 us -> 8.22 us  [permute(): return lax.ppermute(x, ('band', 'col'), pairs)]
    all_to_all x1 -> x2, waiting for transfers between devices: 0.01 us -> 7.83 us  [the longest x1 7.83 us: local(): lax.all_to_all(weighted, 'band', split_axis=0, concat_axis=0, tiled=True)]
    all_to_all x1 -> x2, starting transfers between devices: 3.38 us -> 8.91 us  [the longest x1 5.34 us: local(): lax.all_to_all(weighted, 'band', split_axis=0, concat_axis=0, tiled=True)]
    all_to_all x1, blocking collectives: 11.3 us -> 15.5 us  [local(): lax.all_to_all(rho, ('band', 'col'), split_axis=0, concat_axis=0, tiled=T...]
    unnamed x1 -> x16, local copies, waits for them, and re-layouts: 0.01 us -> 2.19 us
    pallas_call x4 -> x2, Pallas kernels: 1.46 us -> 2.92 us  [the longest x1 1.72 us: left(): pl.pallas_call(left_kernel, out_shape=jax.ShapeDtypeStruct((double, block...]
    reshape x1 -> x0, local copies, waits for them, and re-layouts: 1.41 us -> none  [densities(): gvec_index.reshape(NPW // 256, 256)]
  transfers between devices with their start and end apart: 28 -> 19, of which waited for: 8 -> 5; matrix products, arithmetic and copies ran while one was open for 0% -> 0% of each run, Pallas kernels for 1% -> 3%
where the time goes in v2:
time: 97.9 us; the launch traced here: 97.5 us
  starting transfers between devices  38.3 us (39%)
  Pallas kernels  23.7 us (24%)
  waiting for transfers between devices  16.1 us (16%)
  blocking collectives  15.5 us (16%)
  local copies, waits for them, and re-layouts  2.26 us (2%)
  between operations  1.66 us (2%)
    ppermute x17, starting transfers between devices, permute(): return lax.ppermute(x, ('band', 'col'), pairs)  29.4 us
    all_to_all x1, blocking collectives, local(): lax.all_to_all(rho, ('band', 'col'), split_axis=0, concat_axis=0, tiled=T...  15.5 us
    pallas_call x1, Pallas kernels, densities(): pl.pallas_call(functools.partial(density_kernel, pairs, n_col, col_width)...  14.6 us
    ppermute x17, waiting for transfers between devices, permute(): return lax.ppermute(x, ('band', 'col'), pairs)  8.22 us
    all_to_all x1, waiting for transfers between devices, local(): lax.all_to_all(weighted, 'band', split_axis=0, concat_axis=0, tiled=True)  7.83 us
    pallas_call x1, Pallas kernels, product(): pl.pallas_call(functools.partial(product_kernel, [g[:2] + (len(g[2]),) fo...  6.12 us
    all_to_all x1, starting transfers between devices, local(): lax.all_to_all(weighted, 'band', split_axis=0, concat_axis=0, tiled=True)  5.34 us
    all_to_all x1, starting transfers between devices, local(): rows = lax.all_to_all(rows, 'col', split_axis=0, concat_axis=0, tiled=True)  3.57 us
  transfers between devices with their start and end apart: 19, of which 5 were waited for; matrix products, arithmetic and copies ran while one was open for 0% of the time, Pallas kernels for 3%

profile of v2, /device:TPU:1, one launch (start us, length us, event | category | flops | bytes accessed | tf_op | source)
XLA Modules:
  0.0 97.5 jit_solution(7068012374187885447)
XLA Ops:
  1.3 14.6 %shard_map.100 = (bf16[2,8,8,1280]{3,2,1,0:T(8,128)(2,1)}, bf16[32,8,320]{2,1,0:T(8,128)(2,1)}) custom-call(bf16[1,64,64,128]{3,2,1,0:T(8,128)(2,1)} %v_ref.1, bf16[4,64,64,128]{3,2,1,0:T(8,128)(2,1)} %c_ref.1, bf16[432,512]{1,0:T(8,128)(2,1)} %constant.6.clone.xm_ref, bf16[64,64]{1,0:T(8,128)(2,1)} %constant.7.clone.ym_ref, ...), custom_call_target="tpu_custom_call" | custom-call | flops 2000000000 | bytes 6000000 | tf_op jit(solution)/shard_map/pallas_call | solution.py:195
  15.9 15.5 %all_to_all.15 = bf16[16,8,1280]{2,1,0:T(8,128)(2,1)S(1)} all-to-all(bf16[16,8,1280]{2,1,0:T(8,128)(2,1)} %bitcast.8), channel_id=1, replica_groups={{0,1,2,3,4,5,6,7,16,17,18,19,20,21,22,23},{8,9,10,11,12,13,14,15,24,25,..., dimensions={0} | all-to-all | bytes 655360 | tf_op jit(solution)/shard_map/all_to_all | solution.py:388
  31.4 2.2 %collective-permute-start = (bf16[128,1280]{1,0:T(8,128)(2,1)S(1)}, bf16[128,1280]{1,0:T(8,128)(2,1)S(1)}, u32[]{:S(2)}, u32[]{:S(2)}) collective-permute-start(bf16[128,1280]{1,0:T(8,128)(2,1)S(1)} %bitcast.7), channel_id=1, source_target_pairs={{0,8},{1,9},{2,10},{3,11},{4,12},{5,13},{6,14},{7,15},{8,0},{9,1},... | collective-permute-start | bytes 983048 | tf_op jit(solution)/shard_map/ppermute | solution.py:366
  33.7 1.2 %collective-permute-done = bf16[128,1280]{1,0:T(8,128)(2,1)S(1)} collective-permute-done((bf16[128,1280]{1,0:T(8,128)(2,1)S(1)}, bf16[128,1280]{1,0:T(8,128)(2,1)S(1)}, u32[]{:S(2)}, u32[]{:S(2)}) %collective-permute-start) | collective-permute-done | bytes 327712 | tf_op jit(solution)/shard_map/ppermute | solution.py:366
  35.0 5.7 %collective-permute-start.1 = (bf16[128,1280]{1,0:T(8,128)(2,1)S(1)}, bf16[128,1280]{1,0:T(8,128)(2,1)S(1)}, u32[]{:S(2)}, u32[]{:S(2)}) collective-permute-start(bf16[128,1280]{1,0:T(8,128)(2,1)S(1)} %pad_maximum_fusion.refs_0_), channel_id=1, source_target_pairs={{0,32},{1,33},{2,34},{3,35},{4,36},{5,37},{6,38},{7,39},{8,232},{9... | collective-permute-start | bytes 983048 | tf_op jit(solution)/shard_map/ppermute | solution.py:366
  40.6 5.3 %all-to-all-start = ((bf16[32,8,320]{2,1,0:T(8,128)(2,1)}), bf16[32,8,320]{2,1,0:T(8,128)(2,1)S(1)}, u32[]{:S(2)}, u32[]{:S(2)}) async-start(bf16[32,8,320]{2,1,0:T(8,128)(2,1)} %get-tuple-element.7), calls=%async_computation | async-start | bytes 393216 | tf_op jit(solution)/shard_map/all_to_all | solution.py:398
  45.9 0.0 collective-permute-done.1.refs_2_
  46.0 2.7 %collective-permute-start.2 = (bf16[128,1280]{1,0:T(8,128)(2,1)S(1)}, bf16[128,1280]{1,0:T(8,128)(2,1)S(1)}, u32[]{:S(2)}, u32[]{:S(2)}) collective-permute-start(bf16[128,1280]{1,0:T(8,128)(2,1)S(1)} %collective-permute-done.1.refs_2_), channel_id=1, source_target_pairs={{0,32},{1,33},{2,34},{3,35},{4,36},{5,37},{6,38},{7,39},{8,232},{9... | collective-permute-start | bytes 983048 | tf_op jit(solution)/shard_map/ppermute | solution.py:366
  48.7 1.2 %collective-permute-start.3 = (bf16[128,1280]{1,0:T(8,128)(2,1)S(1)}, bf16[128,1280]{1,0:T(8,128)(2,1)S(1)}, u32[]{:S(2)}, u32[]{:S(2)}) collective-permute-start(bf16[128,1280]{1,0:T(8,128)(2,1)S(1)} %pad_maximum_fusion.1.refs_1_), channel_id=1, source_target_pairs={{0,32},{1,33},{2,34},{3,35},{4,36},{5,37},{6,38},{7,39},{8,232},{9... | collective-permute-start | bytes 983048 | tf_op jit(solution)/shard_map/ppermute | solution.py:366
  50.0 7.8 %all-to-all-done.in_ref = bf16[32,8,320]{2,1,0:T(8,128)(2,1)S(1)} async-done(((bf16[32,8,320]{2,1,0:T(8,128)(2,1)}), bf16[32,8,320]{2,1,0:T(8,128)(2,1)S(1)}, u32[]{:S(2)}, u32[]{:S(2)}) %all-to-all-start) | async-done | bytes 163872 | tf_op jit(solution)/shard_map/all_to_all | solution.py:398
  57.8 0.0 collective-permute-done.2.after_ref.refs_6_
  57.8 1.2 %shard_map.101 = bf16[8,16,8,640]{3,2,1,0:T(8,128)(2,1)} custom-call(bf16[32,8,320]{2,1,0:T(8,128)(2,1)S(1)} %all-to-all-done.in_ref, bf16[128,1280]{1,0:T(8,128)(2,1)S(1)} %collective-permute-done.2.after_ref.refs_6_), custom_call_target="tpu_custom_call" | custom-call | flops 1000 | bytes 1000 | tf_op jit(solution)/shard_map/pallas_call | solution.py:246
  59.0 3.6 %all-to-all-start.2 = ((bf16[8,16,8,640]{3,2,1,0:T(8,128)(2,1)}), bf16[8,16,8,640]{3,2,1,0:T(8,128)(2,1)S(1)}, u32[]{:S(2)}, u32[]{:S(2)}) async-start(bf16[8,16,8,640]{3,2,1,0:T(8,128)(2,1)} %shard_map.101), calls=%async_computation.2 | async-start | bytes 2621440 | tf_op jit(solution)/shard_map/all_to_all | solution.py:402
  62.6 0.0 collective-permute-done.3.refs_3_
  62.6 0.0 copy-start
  62.6 0.1 collective-permute-start.6
  62.7 1.3 %collective-permute-start.9 = (bf16[128,1280]{1,0:T(8,128)(2,1)S(1)}, bf16[128,1280]{1,0:T(8,128)(2,1)S(1)}, u32[]{:S(2)}, u32[]{:S(2)}) collective-permute-start(bf16[128,1280]{1,0:T(8,128)(2,1)S(1)} %collective-permute-done.2.after_ref.refs_6_), channel_id=1, source_target_pairs={{0,32},{1,33},{2,34},{3,35},{4,36},{5,37},{6,38},{7,39},{8,232},{9... | collective-permute-start | bytes 983048 | tf_op jit(solution)/shard_map/ppermute | solution.py:366
  64.0 0.0 copy-done
  64.0 5.0 %collective-permute-done.6.refs_7_ = bf16[128,1280]{1,0:T(8,128)(2,1)} collective-permute-done((bf16[128,1280]{1,0:T(8,128)(2,1)S(1)}, bf16[128,1280]{1,0:T(8,128)(2,1)}, u32[]{:S(2)}, u32[]{:S(2)}) %collective-permute-start.6) | collective-permute-done | bytes 327712 | tf_op jit(solution)/shard_map/ppermute | solution.py:366
  69.0 1.1 %collective-permute-start.10 = (bf16[128,1280]{1,0:T(8,128)(2,1)}, bf16[128,1280]{1,0:T(8,128)(2,1)S(1)}, u32[]{:S(2)}, u32[]{:S(2)}) collective-permute-start(bf16[128,1280]{1,0:T(8,128)(2,1)} %collective-permute-done.6.refs_7_), channel_id=1, source_target_pairs={{0,32},{1,33},{2,34},{3,35},{4,36},{5,37},{6,38},{7,39},{8,232},{9... | collective-permute-start | bytes 983048 | tf_op jit(solution)/shard_map/ppermute | solution.py:366
  70.1 1.8 %collective-permute-start.4 = (bf16[128,1280]{1,0:T(8,128)(2,1)S(1)}, bf16[128,1280]{1,0:T(8,128)(2,1)S(1)}, u32[]{:S(2)}, u32[]{:S(2)}) collective-permute-start(bf16[128,1280]{1,0:T(8,128)(2,1)S(1)} %collective-permute-done.1.refs_2_), channel_id=1, source_target_pairs={{0,8},{1,9},{2,10},{3,11},{4,12},{5,13},{6,14},{7,15},{8,0},{9,1},... | collective-permute-start | bytes 983048 | tf_op jit(solution)/shard_map/ppermute | solution.py:366
  71.9 0.0 collective-permute-start.5
  71.9 0.5 collective-permute-start.7
  72.4 0.0 collective-permute-done.9.refs_10_
  72.4 2.5 %collective-permute-start.8 = (bf16[128,1280]{1,0:T(8,128)(2,1)}, bf16[128,1280]{1,0:T(8,128)(2,1)}, u32[]{:S(2)}, u32[]{:S(2)}) collective-permute-start(bf16[128,1280]{1,0:T(8,128)(2,1)} %collective-permute-done.6.refs_7_), channel_id=1, source_target_pairs={{0,8},{1,9},{2,10},{3,11},{4,12},{5,13},{6,14},{7,15},{8,0},{9,1},... | collective-permute-start | bytes 983048 | tf_op jit(solution)/shard_map/ppermute | solution.py:366
  74.9 1.0 %collective-permute-done.10.refs_11_ = bf16[128,1280]{1,0:T(8,128)(2,1)S(1)} collective-permute-done((bf16[128,1280]{1,0:T(8,128)(2,1)}, bf16[128,1280]{1,0:T(8,128)(2,1)S(1)}, u32[]{:S(2)}, u32[]{:S(2)}) %collective-permute-start.10) | collective-permute-done | bytes 327712 | tf_op jit(solution)/shard_map/ppermute | solution.py:366
  75.9 1.8 %collective-permute-start.13 = (bf16[64,1280]{1,0:T(8,128)(2,1)S(1)}, bf16[64,1280]{1,0:T(8,128)(2,1)S(1)}, u32[]{:S(2)}, u32[]{:S(2)}) collective-permute-start(bf16[64,1280]{1,0:T(8,128)(2,1)S(1)} %slice.36), channel_id=1, source_target_pairs={{0,32},{1,33},{2,34},{3,35},{4,36},{5,37},{6,38},{7,39},{8,232},{9... | collective-permute-start | bytes 491528 | tf_op jit(solution)/shard_map/ppermute | solution.py:366
  77.8 0.0 collective-permute-done.4.refs_4_
  77.8 0.0 copy-start.2
  77.8 0.7 copy-done.2
  78.5 2.2 %collective-permute-start.11 = (bf16[128,1280]{1,0:T(8,128)(2,1)S(1)}, bf16[128,1280]{1,0:T(8,128)(2,1)}, u32[]{:S(2)}, u32[]{:S(2)}) collective-permute-start(bf16[128,1280]{1,0:T(8,128)(2,1)S(1)} %collective-permute-done.9.refs_10_), channel_id=1, source_target_pairs={{0,8},{1,9},{2,10},{3,11},{4,12},{5,13},{6,14},{7,15},{8,0},{9,1},... | collective-permute-start | bytes 983048 | tf_op jit(solution)/shard_map/ppermute | solution.py:366
  80.7 0.0 collective-permute-done.5.refs_5_
  80.7 0.0 copy-start.4
  80.7 0.7 copy-done.4
  81.4 0.0 collective-permute-start.12
  81.4 0.0 collective-permute-done.7.refs_8_
  81.5 0.0 copy-start.6
  81.5 0.7 copy-done.6
  82.2 3.0 %collective-permute-start.15 = (bf16[64,1280]{1,0:T(8,128)(2,1)S(1)}, bf16[64,1280]{1,0:T(8,128)(2,1)}, u32[]{:S(2)}, u32[]{:S(2)}) collective-permute-start(bf16[64,1280]{1,0:T(8,128)(2,1)S(1)} %slice.37), channel_id=1, source_target_pairs={{0,32},{1,33},{2,34},{3,35},{4,36},{5,37},{6,38},{7,39},{8,232},{9... | collective-permute-start | bytes 491528 | tf_op jit(solution)/shard_map/ppermute | solution.py:366
  85.1 0.0 collective-permute-done.13.refs_14_
  85.1 1.3 %collective-permute-start.14 = (bf16[64,1280]{1,0:T(8,128)(2,1)S(1)}, bf16[64,1280]{1,0:T(8,128)(2,1)}, u32[]{:S(2)}, u32[]{:S(2)}) collective-permute-start(bf16[64,1280]{1,0:T(8,128)(2,1)S(1)} %collective-permute-done.13.refs_14_), channel_id=1, source_target_pairs={{0,8},{1,9},{2,10},{3,11},{4,12},{5,13},{6,14},{7,15},{8,0},{9,1},... | collective-permute-start | bytes 491528 | tf_op jit(solution)/shard_map/ppermute | solution.py:366
  86.5 0.9 collective-permute-done.15.refs_16_
  87.4 1.9 %collective-permute-start.16 = (bf16[64,1280]{1,0:T(8,128)(2,1)}, bf16[64,1280]{1,0:T(8,128)(2,1)}, u32[]{:S(2)}, u32[]{:S(2)}) collective-permute-start(bf16[64,1280]{1,0:T(8,128)(2,1)} %collective-permute-done.15.refs_16_), channel_id=1, source_target_pairs={{0,8},{1,9},{2,10},{3,11},{4,12},{5,13},{6,14},{7,15},{8,0},{9,1},... | collective-permute-start | bytes 491528 | tf_op jit(solution)/shard_map/ppermute | solution.py:366
  89.3 0.0 all-to-all-done.2.in_ref
  89.3 0.0 copy-start.1
  89.3 0.0 copy-start.3
  89.3 0.0 copy-start.5
  89.3 0.0 copy-start.7
  89.4 1.7 %shard_map.102.l_ref = bf16[640,2048]{1,0:T(8,128)(2,1)S(1)} custom-call(bf16[8,16,8,640]{3,2,1,0:T(8,128)(2,1)S(1)} %all-to-all-done.2.in_ref), custom_call_target="tpu_custom_call" | custom-call | flops 1000 | bytes 1000 | tf_op jit(solution)/shard_map/pallas_call | solution.py:286
  91.1 0.0 collective-permute-done.8.refs_9_
  91.1 0.0 collective-permute-done.11.refs_12_
  91.1 0.0 collective-permute-done.12.refs_13_
  91.1 0.0 collective-permute-done.14.refs_15_
  91.1 0.0 collective-permute-done.16.refs_17_
  91.1 0.0 copy-done.1
  91.1 0.0 copy-done.3
  91.2 0.0 copy-done.5
  91.2 0.0 copy-done.7
  91.2 6.1 %shard_map.103 = f32[2,320,1280]{2,1,0:T(8,128)} custom-call(bf16[640,2048]{1,0:T(8,128)(2,1)S(1)} %shard_map.102.l_ref, bf16[128,1280]{1,0:T(8,128)(2,1)S(1)} %pad_maximum_fusion.refs_0_, bf16[128,1280]{1,0:T(8,128)(2,1)S(1)} %pad_maximum_fusion.1.refs_1_, bf16[128,1280]{1,0:T(8,128)(2,1)S(1)} %collective-permute-done.1.refs_2_, ...), custom_call_target="tpu_custom_call" | custom-call | flops 1000 | bytes 1000 | tf_op jit(solution)/shard_map/pallas_call | solution.py:346
  (6 shorter events, 0.1 us)
Async XLA Ops:
  31.4 3.5 %collective-permute-start = (bf16[128,1280]{1,0:T(8,128)(2,1)S(1)}, bf16[128,1280]{1,0:T(8,128)(2,1)S(1)}, u32[]{:S(2)}, u32[]{:S(2)}) collective-permute-start(bf16[128,1280]{1,0:T(8,128)(2,1)S(1)} %bitcast.7), channel_id=1, source_target_pairs={{0,8},{1,9},{2,10},{3,11},{4,12},{5,13},{6,14},{7,15},{8,0},{9,1},... | collective-permute-start | bytes 983048 | tf_op jit(solution)/shard_map/ppermute | solution.py:366
  35.0 11.0 %collective-permute-start.1 = (bf16[128,1280]{1,0:T(8,128)(2,1)S(1)}, bf16[128,1280]{1,0:T(8,128)(2,1)S(1)}, u32[]{:S(2)}, u32[]{:S(2)}) collective-permute-start(bf16[128,1280]{1,0:T(8,128)(2,1)S(1)} %pad_maximum_fusion.refs_0_), channel_id=1, source_target_pairs={{0,32},{1,33},{2,34},{3,35},{4,36},{5,37},{6,38},{7,39},{8,232},{9... | collective-permute-start | bytes 983048 | tf_op jit(solution)/shard_map/ppermute | solution.py:366
  40.6 17.2 %all-to-all-start = ((bf16[32,8,320]{2,1,0:T(8,128)(2,1)}), bf16[32,8,320]{2,1,0:T(8,128)(2,1)S(1)}, u32[]{:S(2)}, u32[]{:S(2)}) async-start(bf16[32,8,320]{2,1,0:T(8,128)(2,1)} %get-tuple-element.7), calls=%async_computation | async-start | bytes 393216 | tf_op jit(solution)/shard_map/all_to_all | solution.py:398
  46.0 11.8 %collective-permute-start.2 = (bf16[128,1280]{1,0:T(8,128)(2,1)S(1)}, bf16[128,1280]{1,0:T(8,128)(2,1)S(1)}, u32[]{:S(2)}, u32[]{:S(2)}) collective-permute-start(bf16[128,1280]{1,0:T(8,128)(2,1)S(1)} %collective-permute-done.1.refs_2_), channel_id=1, source_target_pairs={{0,32},{1,33},{2,34},{3,35},{4,36},{5,37},{6,38},{7,39},{8,232},{9... | collective-permute-start | bytes 983048 | tf_op jit(solution)/shard_map/ppermute | solution.py:366
  48.7 13.9 %collective-permute-start.3 = (bf16[128,1280]{1,0:T(8,128)(2,1)S(1)}, bf16[128,1280]{1,0:T(8,128)(2,1)S(1)}, u32[]{:S(2)}, u32[]{:S(2)}) collective-permute-start(bf16[128,1280]{1,0:T(8,128)(2,1)S(1)} %pad_maximum_fusion.1.refs_1_), channel_id=1, source_target_pairs={{0,32},{1,33},{2,34},{3,35},{4,36},{5,37},{6,38},{7,39},{8,232},{9... | collective-permute-start | bytes 983048 | tf_op jit(solution)/shard_map/ppermute | solution.py:366
  59.0 30.3 %all-to-all-start.2 = ((bf16[8,16,8,640]{3,2,1,0:T(8,128)(2,1)}), bf16[8,16,8,640]{3,2,1,0:T(8,128)(2,1)S(1)}, u32[]{:S(2)}, u32[]{:S(2)}) async-start(bf16[8,16,8,640]{3,2,1,0:T(8,128)(2,1)} %shard_map.101), calls=%async_computation.2 | async-start | bytes 2621440 | tf_op jit(solution)/shard_map/all_to_all | solution.py:402
  62.6 1.4 %copy-start = (bf16[128,1280]{1,0:T(8,128)(2,1)}, bf16[128,1280]{1,0:T(8,128)(2,1)S(1)}, u32[]{:S(2)}) copy-start(bf16[128,1280]{1,0:T(8,128)(2,1)S(1)} %collective-permute-done.3.refs_3_) | copy-start | bytes 983044
  62.6 6.4 %collective-permute-start.6 = (bf16[128,1280]{1,0:T(8,128)(2,1)S(1)}, bf16[128,1280]{1,0:T(8,128)(2,1)}, u32[]{:S(2)}, u32[]{:S(2)}) collective-permute-start(bf16[128,1280]{1,0:T(8,128)(2,1)S(1)} %collective-permute-done.3.refs_3_), channel_id=1, source_target_pairs={{0,32},{1,33},{2,34},{3,35},{4,36},{5,37},{6,38},{7,39},{8,232},{9... | collective-permute-start | bytes 983048 | tf_op jit(solution)/shard_map/ppermute | solution.py:366
  62.7 9.7 %collective-permute-start.9 = (bf16[128,1280]{1,0:T(8,128)(2,1)S(1)}, bf16[128,1280]{1,0:T(8,128)(2,1)S(1)}, u32[]{:S(2)}, u32[]{:S(2)}) collective-permute-start(bf16[128,1280]{1,0:T(8,128)(2,1)S(1)} %collective-permute-done.2.after_ref.refs_6_), channel_id=1, source_target_pairs={{0,32},{1,33},{2,34},{3,35},{4,36},{5,37},{6,38},{7,39},{8,232},{9... | collective-permute-start | bytes 983048 | tf_op jit(solution)/shard_map/ppermute | solution.py:366
  69.0 6.9 %collective-permute-start.10 = (bf16[128,1280]{1,0:T(8,128)(2,1)}, bf16[128,1280]{1,0:T(8,128)(2,1)S(1)}, u32[]{:S(2)}, u32[]{:S(2)}) collective-permute-start(bf16[128,1280]{1,0:T(8,128)(2,1)} %collective-permute-done.6.refs_7_), channel_id=1, source_target_pairs={{0,32},{1,33},{2,34},{3,35},{4,36},{5,37},{6,38},{7,39},{8,232},{9... | collective-permute-start | bytes 983048 | tf_op jit(solution)/shard_map/ppermute | solution.py:366
  70.1 7.7 %collective-permute-start.4 = (bf16[128,1280]{1,0:T(8,128)(2,1)S(1)}, bf16[128,1280]{1,0:T(8,128)(2,1)S(1)}, u32[]{:S(2)}, u32[]{:S(2)}) collective-permute-start(bf16[128,1280]{1,0:T(8,128)(2,1)S(1)} %collective-permute-done.1.refs_2_), channel_id=1, source_target_pairs={{0,8},{1,9},{2,10},{3,11},{4,12},{5,13},{6,14},{7,15},{8,0},{9,1},... | collective-permute-start | bytes 983048 | tf_op jit(solution)/shard_map/ppermute | solution.py:366
  71.9 8.8 %collective-permute-start.5 = (bf16[128,1280]{1,0:T(8,128)(2,1)}, bf16[128,1280]{1,0:T(8,128)(2,1)S(1)}, u32[]{:S(2)}, u32[]{:S(2)}) collective-permute-start(bf16[128,1280]{1,0:T(8,128)(2,1)} %copy-done), channel_id=1, source_target_pairs={{0,8},{1,9},{2,10},{3,11},{4,12},{5,13},{6,14},{7,15},{8,0},{9,1},... | collective-permute-start | bytes 983048 | tf_op jit(solution)/shard_map/ppermute | solution.py:366
  71.9 9.6 %collective-permute-start.7 = (bf16[128,1280]{1,0:T(8,128)(2,1)S(1)}, bf16[128,1280]{1,0:T(8,128)(2,1)S(1)}, u32[]{:S(2)}, u32[]{:S(2)}) collective-permute-start(bf16[128,1280]{1,0:T(8,128)(2,1)S(1)} %collective-permute-done.2.after_ref.refs_6_), channel_id=1, source_target_pairs={{0,8},{1,9},{2,10},{3,11},{4,12},{5,13},{6,14},{7,15},{8,0},{9,1},... | collective-permute-start | bytes 983048 | tf_op jit(solution)/shard_map/ppermute | solution.py:366
  72.4 18.7 %collective-permute-start.8 = (bf16[128,1280]{1,0:T(8,128)(2,1)}, bf16[128,1280]{1,0:T(8,128)(2,1)}, u32[]{:S(2)}, u32[]{:S(2)}) collective-permute-start(bf16[128,1280]{1,0:T(8,128)(2,1)} %collective-permute-done.6.refs_7_), channel_id=1, source_target_pairs={{0,8},{1,9},{2,10},{3,11},{4,12},{5,13},{6,14},{7,15},{8,0},{9,1},... | collective-permute-start | bytes 983048 | tf_op jit(solution)/shard_map/ppermute | solution.py:366
  75.9 9.2 %collective-permute-start.13 = (bf16[64,1280]{1,0:T(8,128)(2,1)S(1)}, bf16[64,1280]{1,0:T(8,128)(2,1)S(1)}, u32[]{:S(2)}, u32[]{:S(2)}) collective-permute-start(bf16[64,1280]{1,0:T(8,128)(2,1)S(1)} %slice.36), channel_id=1, source_target_pairs={{0,32},{1,33},{2,34},{3,35},{4,36},{5,37},{6,38},{7,39},{8,232},{9... | collective-permute-start | bytes 491528 | tf_op jit(solution)/shard_map/ppermute | solution.py:366
  77.8 0.7 copy-start.2
  78.5 12.6 %collective-permute-start.11 = (bf16[128,1280]{1,0:T(8,128)(2,1)S(1)}, bf16[128,1280]{1,0:T(8,128)(2,1)}, u32[]{:S(2)}, u32[]{:S(2)}) collective-permute-start(bf16[128,1280]{1,0:T(8,128)(2,1)S(1)} %collective-permute-done.9.refs_10_), channel_id=1, source_target_pairs={{0,8},{1,9},{2,10},{3,11},{4,12},{5,13},{6,14},{7,15},{8,0},{9,1},... | collective-permute-start | bytes 983048 | tf_op jit(solution)/shard_map/ppermute | solution.py:366
  80.7 0.7 copy-start.4
  81.4 9.7 %collective-permute-start.12 = (bf16[128,1280]{1,0:T(8,128)(2,1)S(1)}, bf16[128,1280]{1,0:T(8,128)(2,1)}, u32[]{:S(2)}, u32[]{:S(2)}) collective-permute-start(bf16[128,1280]{1,0:T(8,128)(2,1)S(1)} %collective-permute-done.10.refs_11_), channel_id=1, source_target_pairs={{0,8},{1,9},{2,10},{3,11},{4,12},{5,13},{6,14},{7,15},{8,0},{9,1},... | collective-permute-start | bytes 983048 | tf_op jit(solution)/shard_map/ppermute | solution.py:366
  81.5 0.7 copy-start.6
  82.2 5.2 %collective-permute-start.15 = (bf16[64,1280]{1,0:T(8,128)(2,1)S(1)}, bf16[64,1280]{1,0:T(8,128)(2,1)}, u32[]{:S(2)}, u32[]{:S(2)}) collective-permute-start(bf16[64,1280]{1,0:T(8,128)(2,1)S(1)} %slice.37), channel_id=1, source_target_pairs={{0,32},{1,33},{2,34},{3,35},{4,36},{5,37},{6,38},{7,39},{8,232},{9... | collective-permute-start | bytes 491528 | tf_op jit(solution)/shard_map/ppermute | solution.py:366
  85.1 6.0 %collective-permute-start.14 = (bf16[64,1280]{1,0:T(8,128)(2,1)S(1)}, bf16[64,1280]{1,0:T(8,128)(2,1)}, u32[]{:S(2)}, u32[]{:S(2)}) collective-permute-start(bf16[64,1280]{1,0:T(8,128)(2,1)S(1)} %collective-permute-done.13.refs_14_), channel_id=1, source_target_pairs={{0,8},{1,9},{2,10},{3,11},{4,12},{5,13},{6,14},{7,15},{8,0},{9,1},... | collective-permute-start | bytes 491528 | tf_op jit(solution)/shard_map/ppermute | solution.py:366
  87.4 3.7 %collective-permute-start.16 = (bf16[64,1280]{1,0:T(8,128)(2,1)}, bf16[64,1280]{1,0:T(8,128)(2,1)}, u32[]{:S(2)}, u32[]{:S(2)}) collective-permute-start(bf16[64,1280]{1,0:T(8,128)(2,1)} %collective-permute-done.15.refs_16_), channel_id=1, source_target_pairs={{0,8},{1,9},{2,10},{3,11},{4,12},{5,13},{6,14},{7,15},{8,0},{9,1},... | collective-permute-start | bytes 491528 | tf_op jit(solution)/shard_map/ppermute | solution.py:366
  89.3 1.8 %copy-start.1 = (bf16[128,1280]{1,0:T(8,128)(2,1)S(1)}, bf16[128,1280]{1,0:T(8,128)(2,1)}, u32[]{:S(2)}) copy-start(bf16[128,1280]{1,0:T(8,128)(2,1)} %copy-done) | copy-start | bytes 983044
  89.3 1.8 %copy-start.3 = (bf16[128,1280]{1,0:T(8,128)(2,1)S(1)}, bf16[128,1280]{1,0:T(8,128)(2,1)}, u32[]{:S(2)}) copy-start(bf16[128,1280]{1,0:T(8,128)(2,1)} %copy-done.2) | copy-start | bytes 983044
  89.3 1.8 %copy-start.5 = (bf16[128,1280]{1,0:T(8,128)(2,1)S(1)}, bf16[128,1280]{1,0:T(8,128)(2,1)}, u32[]{:S(2)}) copy-start(bf16[128,1280]{1,0:T(8,128)(2,1)} %copy-done.4) | copy-start | bytes 983044
  89.3 1.8 %copy-start.7 = (bf16[128,1280]{1,0:T(8,128)(2,1)S(1)}, bf16[128,1280]{1,0:T(8,128)(2,1)}, u32[]{:S(2)}) copy-start(bf16[128,1280]{1,0:T(8,128)(2,1)} %copy-done.6) | copy-start | bytes 983044

commit v3 on v2

--- a/solution.py
+++ b/solution.py
@@ -22,10 +22,11 @@
     axis = (np.arange(NG) + NG // 2) % NG - NG // 2
     square = axis * axis
     length = np.sort((square[:, None, None] + square[None, :, None] + square[None, None, :]).ravel())
-    return int(length[NPW - 1])
-
-
-LIMIT = sphere_radius()
+    return length[:NPW]
+
+
+LENGTHS = sphere_radius()
+LIMIT = int(LENGTHS[NPW - 1])
 KMAX = math.isqrt(LIMIT)
 KS = list(range(-KMAX, KMAX + 1))
 NK = len(KS)
@@ -80,6 +81,29 @@
 
 def signed(index):
     return ((index + NG // 2) & (NG - 1)) - NG // 2
+
+
+def spans(dests, width):
+    runs = []
+    for dest in range(dests):
+        kmax = math.isqrt(int(LENGTHS[(dest + 1) * width - 1]))
+        low = BASE[KMAX - kmax]
+        high = BASE[KMAX + kmax] + rows_for(kmax)
+        size = -(-(high - low) // 128) * 128
+        if size < 512:
+            size = 512
+        if size > 640 or low + size > ROWS:
+            low, size = 0, ROWS
+        runs.append((low, low + size))
+    merged = []
+    for dest, run in enumerate(runs):
+        if merged and merged[-1][0][1] - merged[-1][0][0] == run[1] - run[0]:
+            old = merged[-1]
+            wide = run if run[0] <= old[0][0] else old[0]
+            merged[-1] = (wide, old[1], dest + 1)
+        else:
+            merged.append((run, dest, dest + 1))
+    return merged
 
 
 def wide_row(ref, which):
@@ -145,16 +169,15 @@
             place = jnp.where(comp_x == kx, place + BASE[i], place)
         pos_ref[...] = place
         kz_ref[...] = signed(index & (NG - 1)) + KMAX
-        row_id = lax.broadcasted_iota(jnp.int32, (ROWS, 256), 0)
         blocks = col_width // 256
 
-        def body(dest, carry):
+        def body(low, table, row_id, dest, carry):
             for k in range(blocks):
                 which = dest * blocks + k
                 pos = wide_row(pos_ref, which)
                 kz = wide_row(kz_ref, which)
-                pick = jnp.where(row_id == pos, 1.0, 0.0).astype(jnp.bfloat16)
-                found = jnp.dot(third, pick, preferred_element_type=jnp.float32)
+                pick = jnp.where(row_id == pos - low, 1.0, 0.0).astype(jnp.bfloat16)
+                found = jnp.dot(table, pick, preferred_element_type=jnp.float32)
                 found = found.reshape(NK, 2 * pairs, 256)
                 acc = jnp.zeros((2 * pairs, 256), jnp.float32)
                 for i in range(NK):
@@ -164,7 +187,10 @@
                 flat_ref[which] = acc
             return carry
 
-        lax.fori_loop(0, dests, body, 0)
+        for (low, high), first, end in spans(dests, col_width):
+            table = third[:, low:high]
+            row_id = lax.broadcasted_iota(jnp.int32, (high - low, 256), 0)
+            lax.fori_loop(first, end, functools.partial(body, low, table, row_id), 0)
         which_pair = lax.broadcasted_iota(jnp.int32, (2 * pairs, 128), 0) % pairs
         occ_diff = jnp.zeros((2 * pairs, 128), jnp.float32)
         energy = jnp.ones((2 * pairs, 128), jnp.float32)

time: 97.9 us -> 97.6 us (level)
  no operation moved by 1% of the time
where the time goes in v3:
time: 97.6 us; the launch traced here: 97.2 us
  starting transfers between devices  38.3 us (39%)
  Pallas kernels  23.4 us (24%)
  waiting for transfers between devices  16.1 us (16%)
  blocking collectives  15.5 us (16%)
  local copies, waits for them, and re-layouts  2.26 us (2%)
  between operations  1.66 us (2%)
    ppermute x17, starting transfers between devices, permute(): return lax.ppermute(x, ('band', 'col'), pairs)  29.4 us
    all_to_all x1, blocking collectives, local(): lax.all_to_all(rho, ('band', 'col'), split_axis=0, concat_axis=0, tiled=T...  15.5 us
    pallas_call x1, Pallas kernels, densities(): pl.pallas_call(functools.partial(density_kernel, pairs, n_col, col_width)...  14.4 us
    ppermute x17, waiting for transfers between devices, permute(): return lax.ppermute(x, ('band', 'col'), pairs)  8.22 us
    all_to_all x1, waiting for transfers between devices, local(): lax.all_to_all(weighted, 'band', split_axis=0, concat_axis=0, tiled=True)  7.83 us
    pallas_call x1, Pallas kernels, product(): pl.pallas_call(functools.partial(product_kernel, [g[:2] + (len(g[2]),) fo...  6.12 us
    all_to_all x1, starting transfers between devices, local(): lax.all_to_all(weighted, 'band', split_axis=0, concat_axis=0, tiled=True)  5.33 us
    all_to_all x1, starting transfers between devices, local(): rows = lax.all_to_all(rows, 'col', split_axis=0, concat_axis=0, tiled=True)  3.57 us
  transfers between devices with their start and end apart: 19, of which 5 were waited for; matrix products, arithmetic and copies ran while one was open for 0% of the time, Pallas kernels for 3%

profile of v3, /device:TPU:1, one launch (start us, length us, event | category | flops | bytes accessed | tf_op | source)
XLA Modules:
  0.0 97.2 jit_solution(4567592258974036467)
XLA Ops:
  1.3 14.4 %shard_map.100 = (bf16[2,8,8,1280]{3,2,1,0:T(8,128)(2,1)}, bf16[32,8,320]{2,1,0:T(8,128)(2,1)}) custom-call(bf16[1,64,64,128]{3,2,1,0:T(8,128)(2,1)} %v_ref.1, bf16[4,64,64,128]{3,2,1,0:T(8,128)(2,1)} %c_ref.1, bf16[432,512]{1,0:T(8,128)(2,1)} %constant.6.clone.xm_ref, bf16[64,64]{1,0:T(8,128)(2,1)} %constant.7.clone.ym_ref, ...), custom_call_target="tpu_custom_call" | custom-call | flops 2000000000 | bytes 6000000 | tf_op jit(solution)/shard_map/pallas_call | solution.py:221
  15.7 15.5 %all_to_all.15 = bf16[16,8,1280]{2,1,0:T(8,128)(2,1)S(1)} all-to-all(bf16[16,8,1280]{2,1,0:T(8,128)(2,1)} %bitcast.8), channel_id=1, replica_groups={{0,1,2,3,4,5,6,7,16,17,18,19,20,21,22,23},{8,9,10,11,12,13,14,15,24,25,..., dimensions={0} | all-to-all | bytes 655360 | tf_op jit(solution)/shard_map/all_to_all | solution.py:414
  31.1 2.2 %collective-permute-start = (bf16[128,1280]{1,0:T(8,128)(2,1)S(1)}, bf16[128,1280]{1,0:T(8,128)(2,1)S(1)}, u32[]{:S(2)}, u32[]{:S(2)}) collective-permute-start(bf16[128,1280]{1,0:T(8,128)(2,1)S(1)} %bitcast.7), channel_id=1, source_target_pairs={{0,8},{1,9},{2,10},{3,11},{4,12},{5,13},{6,14},{7,15},{8,0},{9,1},... | collective-permute-start | bytes 983048 | tf_op jit(solution)/shard_map/ppermute | solution.py:392
  33.4 1.2 %collective-permute-done = bf16[128,1280]{1,0:T(8,128)(2,1)S(1)} collective-permute-done((bf16[128,1280]{1,0:T(8,128)(2,1)S(1)}, bf16[128,1280]{1,0:T(8,128)(2,1)S(1)}, u32[]{:S(2)}, u32[]{:S(2)}) %collective-permute-start) | collective-permute-done | bytes 327712 | tf_op jit(solution)/shard_map/ppermute | solution.py:392
  34.7 5.7 %collective-permute-start.1 = (bf16[128,1280]{1,0:T(8,128)(2,1)S(1)}, bf16[128,1280]{1,0:T(8,128)(2,1)S(1)}, u32[]{:S(2)}, u32[]{:S(2)}) collective-permute-start(bf16[128,1280]{1,0:T(8,128)(2,1)S(1)} %pad_maximum_fusion.refs_0_), channel_id=1, source_target_pairs={{0,32},{1,33},{2,34},{3,35},{4,36},{5,37},{6,38},{7,39},{8,232},{9... | collective-permute-start | bytes 983048 | tf_op jit(solution)/shard_map/ppermute | solution.py:392
  40.3 5.3 %all-to-all-start = ((bf16[32,8,320]{2,1,0:T(8,128)(2,1)}), bf16[32,8,320]{2,1,0:T(8,128)(2,1)S(1)}, u32[]{:S(2)}, u32[]{:S(2)}) async-start(bf16[32,8,320]{2,1,0:T(8,128)(2,1)} %get-tuple-element.7), calls=%async_computation | async-start | bytes 393216 | tf_op jit(solution)/shard_map/all_to_all | solution.py:424
  45.7 0.0 collective-permute-done.1.refs_2_
  45.7 2.7 %collective-permute-start.2 = (bf16[128,1280]{1,0:T(8,128)(2,1)S(1)}, bf16[128,1280]{1,0:T(8,128)(2,1)S(1)}, u32[]{:S(2)}, u32[]{:S(2)}) collective-permute-start(bf16[128,1280]{1,0:T(8,128)(2,1)S(1)} %collective-permute-done.1.refs_2_), channel_id=1, source_target_pairs={{0,32},{1,33},{2,34},{3,35},{4,36},{5,37},{6,38},{7,39},{8,232},{9... | collective-permute-start | bytes 983048 | tf_op jit(solution)/shard_map/ppermute | solution.py:392
  48.5 1.2 %collective-permute-start.3 = (bf16[128,1280]{1,0:T(8,128)(2,1)S(1)}, bf16[128,1280]{1,0:T(8,128)(2,1)S(1)}, u32[]{:S(2)}, u32[]{:S(2)}) collective-permute-start(bf16[128,1280]{1,0:T(8,128)(2,1)S(1)} %pad_maximum_fusion.1.refs_1_), channel_id=1, source_target_pairs={{0,32},{1,33},{2,34},{3,35},{4,36},{5,37},{6,38},{7,39},{8,232},{9... | collective-permute-start | bytes 983048 | tf_op jit(solution)/shard_map/ppermute | solution.py:392
  49.7 7.8 %all-to-all-done.in_ref = bf16[32,8,320]{2,1,0:T(8,128)(2,1)S(1)} async-done(((bf16[32,8,320]{2,1,0:T(8,128)(2,1)}), bf16[32,8,320]{2,1,0:T(8,128)(2,1)S(1)}, u32[]{:S(2)}, u32[]{:S(2)}) %all-to-all-start) | async-done | bytes 163872 | tf_op jit(solution)/shard_map/all_to_all | solution.py:424
  57.5 0.0 collective-permute-done.2.after_ref.refs_6_
  57.5 1.2 %shard_map.101 = bf16[8,16,8,640]{3,2,1,0:T(8,128)(2,1)} custom-call(bf16[32,8,320]{2,1,0:T(8,128)(2,1)S(1)} %all-to-all-done.in_ref, bf16[128,1280]{1,0:T(8,128)(2,1)S(1)} %collective-permute-done.2.after_ref.refs_6_), custom_call_target="tpu_custom_call" | custom-call | flops 1000 | bytes 1000 | tf_op jit(solution)/shard_map/pallas_call | solution.py:272
  58.7 3.6 %all-to-all-start.2 = ((bf16[8,16,8,640]{3,2,1,0:T(8,128)(2,1)}), bf16[8,16,8,640]{3,2,1,0:T(8,128)(2,1)S(1)}, u32[]{:S(2)}, u32[]{:S(2)}) async-start(bf16[8,16,8,640]{3,2,1,0:T(8,128)(2,1)} %shard_map.101), calls=%async_computation.2 | async-start | bytes 2621440 | tf_op jit(solution)/shard_map/all_to_all | solution.py:428
  62.3 0.0 collective-permute-done.3.refs_3_
  62.3 0.0 copy-start
  62.3 0.1 collective-permute-start.6
  62.4 1.3 %collective-permute-start.9 = (bf16[128,1280]{1,0:T(8,128)(2,1)S(1)}, bf16[128,1280]{1,0:T(8,128)(2,1)S(1)}, u32[]{:S(2)}, u32[]{:S(2)}) collective-permute-start(bf16[128,1280]{1,0:T(8,128)(2,1)S(1)} %collective-permute-done.2.after_ref.refs_6_), channel_id=1, source_target_pairs={{0,32},{1,33},{2,34},{3,35},{4,36},{5,37},{6,38},{7,39},{8,232},{9... | collective-permute-start | bytes 983048 | tf_op jit(solution)/shard_map/ppermute | solution.py:392
  63.7 0.0 copy-done
  63.7 5.0 %collective-permute-done.6.refs_7_ = bf16[128,1280]{1,0:T(8,128)(2,1)} collective-permute-done((bf16[128,1280]{1,0:T(8,128)(2,1)S(1)}, bf16[128,1280]{1,0:T(8,128)(2,1)}, u32[]{:S(2)}, u32[]{:S(2)}) %collective-permute-start.6) | collective-permute-done | bytes 327712 | tf_op jit(solution)/shard_map/ppermute | solution.py:392
  68.7 1.1 %collective-permute-start.10 = (bf16[128,1280]{1,0:T(8,128)(2,1)}, bf16[128,1280]{1,0:T(8,128)(2,1)S(1)}, u32[]{:S(2)}, u32[]{:S(2)}) collective-permute-start(bf16[128,1280]{1,0:T(8,128)(2,1)} %collective-permute-done.6.refs_7_), channel_id=1, source_target_pairs={{0,32},{1,33},{2,34},{3,35},{4,36},{5,37},{6,38},{7,39},{8,232},{9... | collective-permute-start | bytes 983048 | tf_op jit(solution)/shard_map/ppermute | solution.py:392
  69.9 1.8 %collective-permute-start.4 = (bf16[128,1280]{1,0:T(8,128)(2,1)S(1)}, bf16[128,1280]{1,0:T(8,128)(2,1)S(1)}, u32[]{:S(2)}, u32[]{:S(2)}) collective-permute-start(bf16[128,1280]{1,0:T(8,128)(2,1)S(1)} %collective-permute-done.1.refs_2_), channel_id=1, source_target_pairs={{0,8},{1,9},{2,10},{3,11},{4,12},{5,13},{6,14},{7,15},{8,0},{9,1},... | collective-permute-start | bytes 983048 | tf_op jit(solution)/shard_map/ppermute | solution.py:392
  71.6 0.0 collective-permute-start.5
  71.6 0.5 collective-permute-start.7
  72.1 0.0 collective-permute-done.9.refs_10_
  72.1 2.5 %collective-permute-start.8 = (bf16[128,1280]{1,0:T(8,128)(2,1)}, bf16[128,1280]{1,0:T(8,128)(2,1)}, u32[]{:S(2)}, u32[]{:S(2)}) collective-permute-start(bf16[128,1280]{1,0:T(8,128)(2,1)} %collective-permute-done.6.refs_7_), channel_id=1, source_target_pairs={{0,8},{1,9},{2,10},{3,11},{4,12},{5,13},{6,14},{7,15},{8,0},{9,1},... | collective-permute-start | bytes 983048 | tf_op jit(solution)/shard_map/ppermute | solution.py:392
  74.6 1.0 %collective-permute-done.10.refs_11_ = bf16[128,1280]{1,0:T(8,128)(2,1)S(1)} collective-permute-done((bf16[128,1280]{1,0:T(8,128)(2,1)}, bf16[128,1280]{1,0:T(8,128)(2,1)S(1)}, u32[]{:S(2)}, u32[]{:S(2)}) %collective-permute-start.10) | collective-permute-done | bytes 327712 | tf_op jit(solution)/shard_map/ppermute | solution.py:392
  75.7 1.8 %collective-permute-start.13 = (bf16[64,1280]{1,0:T(8,128)(2,1)S(1)}, bf16[64,1280]{1,0:T(8,128)(2,1)S(1)}, u32[]{:S(2)}, u32[]{:S(2)}) collective-permute-start(bf16[64,1280]{1,0:T(8,128)(2,1)S(1)} %slice.36), channel_id=1, source_target_pairs={{0,32},{1,33},{2,34},{3,35},{4,36},{5,37},{6,38},{7,39},{8,232},{9... | collective-permute-start | bytes 491528 | tf_op jit(solution)/shard_map/ppermute | solution.py:392
  77.5 0.0 collective-permute-done.4.refs_4_
  77.5 0.0 copy-start.2
  77.5 0.7 copy-done.2
  78.2 2.2 %collective-permute-start.11 = (bf16[128,1280]{1,0:T(8,128)(2,1)S(1)}, bf16[128,1280]{1,0:T(8,128)(2,1)}, u32[]{:S(2)}, u32[]{:S(2)}) collective-permute-start(bf16[128,1280]{1,0:T(8,128)(2,1)S(1)} %collective-permute-done.9.refs_10_), channel_id=1, source_target_pairs={{0,8},{1,9},{2,10},{3,11},{4,12},{5,13},{6,14},{7,15},{8,0},{9,1},... | collective-permute-start | bytes 983048 | tf_op jit(solution)/shard_map/ppermute | solution.py:392
  80.5 0.0 collective-permute-done.5.refs_5_
  80.5 0.0 copy-start.4
  80.5 0.7 copy-done.4
  81.2 0.0 collective-permute-start.12
  81.2 0.0 collective-permute-done.7.refs_8_
  81.2 0.0 copy-start.6
  81.2 0.7 copy-done.6
  81.9 3.0 %collective-permute-start.15 = (bf16[64,1280]{1,0:T(8,128)(2,1)S(1)}, bf16[64,1280]{1,0:T(8,128)(2,1)}, u32[]{:S(2)}, u32[]{:S(2)}) collective-permute-start(bf16[64,1280]{1,0:T(8,128)(2,1)S(1)} %slice.37), channel_id=1, source_target_pairs={{0,32},{1,33},{2,34},{3,35},{4,36},{5,37},{6,38},{7,39},{8,232},{9... | collective-permute-start | bytes 491528 | tf_op jit(solution)/shard_map/ppermute | solution.py:392
  84.9 0.0 collective-permute-done.13.refs_14_
  84.9 1.4 %collective-permute-start.14 = (bf16[64,1280]{1,0:T(8,128)(2,1)S(1)}, bf16[64,1280]{1,0:T(8,128)(2,1)}, u32[]{:S(2)}, u32[]{:S(2)}) collective-permute-start(bf16[64,1280]{1,0:T(8,128)(2,1)S(1)} %collective-permute-done.13.refs_14_), channel_id=1, source_target_pairs={{0,8},{1,9},{2,10},{3,11},{4,12},{5,13},{6,14},{7,15},{8,0},{9,1},... | collective-permute-start | bytes 491528 | tf_op jit(solution)/shard_map/ppermute | solution.py:392
  86.2 0.9 collective-permute-done.15.refs_16_
  87.1 1.9 %collective-permute-start.16 = (bf16[64,1280]{1,0:T(8,128)(2,1)}, bf16[64,1280]{1,0:T(8,128)(2,1)}, u32[]{:S(2)}, u32[]{:S(2)}) collective-permute-start(bf16[64,1280]{1,0:T(8,128)(2,1)} %collective-permute-done.15.refs_16_), channel_id=1, source_target_pairs={{0,8},{1,9},{2,10},{3,11},{4,12},{5,13},{6,14},{7,15},{8,0},{9,1},... | collective-permute-start | bytes 491528 | tf_op jit(solution)/shard_map/ppermute | solution.py:392
  89.1 0.0 all-to-all-done.2.in_ref
  89.1 0.0 copy-start.1
  89.1 0.0 copy-start.3
  89.1 0.0 copy-start.5
  89.1 0.0 copy-start.7
  89.1 1.7 %shard_map.102.l_ref = bf16[640,2048]{1,0:T(8,128)(2,1)S(1)} custom-call(bf16[8,16,8,640]{3,2,1,0:T(8,128)(2,1)S(1)} %all-to-all-done.2.in_ref), custom_call_target="tpu_custom_call" | custom-call | flops 1000 | bytes 1000 | tf_op jit(solution)/shard_map/pallas_call | solution.py:312
  90.8 0.0 collective-permute-done.8.refs_9_
  90.8 0.0 collective-permute-done.11.refs_12_
  90.8 0.0 collective-permute-done.12.refs_13_
  90.8 0.0 collective-permute-done.14.refs_15_
  90.9 0.0 collective-permute-done.16.refs_17_
  90.9 0.0 copy-done.1
  90.9 0.0 copy-done.3
  90.9 0.0 copy-done.5
  90.9 0.0 copy-done.7
  90.9 6.1 %shard_map.103 = f32[2,320,1280]{2,1,0:T(8,128)} custom-call(bf16[640,2048]{1,0:T(8,128)(2,1)S(1)} %shard_map.102.l_ref, bf16[128,1280]{1,0:T(8,128)(2,1)S(1)} %pad_maximum_fusion.refs_0_, bf16[128,1280]{1,0:T(8,128)(2,1)S(1)} %pad_maximum_fusion.1.refs_1_, bf16[128,1280]{1,0:T(8,128)(2,1)S(1)} %collective-permute-done.1.refs_2_, ...), custom_call_target="tpu_custom_call" | custom-call | flops 1000 | bytes 1000 | tf_op jit(solution)/shard_map/pallas_call | solution.py:372
  (6 shorter events, 0.1 us)
Async XLA Ops:
  31.1 3.5 %collective-permute-start = (bf16[128,1280]{1,0:T(8,128)(2,1)S(1)}, bf16[128,1280]{1,0:T(8,128)(2,1)S(1)}, u32[]{:S(2)}, u32[]{:S(2)}) collective-permute-start(bf16[128,1280]{1,0:T(8,128)(2,1)S(1)} %bitcast.7), channel_id=1, source_target_pairs={{0,8},{1,9},{2,10},{3,11},{4,12},{5,13},{6,14},{7,15},{8,0},{9,1},... | collective-permute-start | bytes 983048 | tf_op jit(solution)/shard_map/ppermute | solution.py:392
  34.7 11.0 %collective-permute-start.1 = (bf16[128,1280]{1,0:T(8,128)(2,1)S(1)}, bf16[128,1280]{1,0:T(8,128)(2,1)S(1)}, u32[]{:S(2)}, u32[]{:S(2)}) collective-permute-start(bf16[128,1280]{1,0:T(8,128)(2,1)S(1)} %pad_maximum_fusion.refs_0_), channel_id=1, source_target_pairs={{0,32},{1,33},{2,34},{3,35},{4,36},{5,37},{6,38},{7,39},{8,232},{9... | collective-permute-start | bytes 983048 | tf_op jit(solution)/shard_map/ppermute | solution.py:392
  40.3 17.2 %all-to-all-start = ((bf16[32,8,320]{2,1,0:T(8,128)(2,1)}), bf16[32,8,320]{2,1,0:T(8,128)(2,1)S(1)}, u32[]{:S(2)}, u32[]{:S(2)}) async-start(bf16[32,8,320]{2,1,0:T(8,128)(2,1)} %get-tuple-element.7), calls=%async_computation | async-start | bytes 393216 | tf_op jit(solution)/shard_map/all_to_all | solution.py:424
  45.7 11.8 %collective-permute-start.2 = (bf16[128,1280]{1,0:T(8,128)(2,1)S(1)}, bf16[128,1280]{1,0:T(8,128)(2,1)S(1)}, u32[]{:S(2)}, u32[]{:S(2)}) collective-permute-start(bf16[128,1280]{1,0:T(8,128)(2,1)S(1)} %collective-permute-done.1.refs_2_), channel_id=1, source_target_pairs={{0,32},{1,33},{2,34},{3,35},{4,36},{5,37},{6,38},{7,39},{8,232},{9... | collective-permute-start | bytes 983048 | tf_op jit(solution)/shard_map/ppermute | solution.py:392
  48.5 13.9 %collective-permute-start.3 = (bf16[128,1280]{1,0:T(8,128)(2,1)S(1)}, bf16[128,1280]{1,0:T(8,128)(2,1)S(1)}, u32[]{:S(2)}, u32[]{:S(2)}) collective-permute-start(bf16[128,1280]{1,0:T(8,128)(2,1)S(1)} %pad_maximum_fusion.1.refs_1_), channel_id=1, source_target_pairs={{0,32},{1,33},{2,34},{3,35},{4,36},{5,37},{6,38},{7,39},{8,232},{9... | collective-permute-start | bytes 983048 | tf_op jit(solution)/shard_map/ppermute | solution.py:392
  58.7 30.3 %all-to-all-start.2 = ((bf16[8,16,8,640]{3,2,1,0:T(8,128)(2,1)}), bf16[8,16,8,640]{3,2,1,0:T(8,128)(2,1)S(1)}, u32[]{:S(2)}, u32[]{:S(2)}) async-start(bf16[8,16,8,640]{3,2,1,0:T(8,128)(2,1)} %shard_map.101), calls=%async_computation.2 | async-start | bytes 2621440 | tf_op jit(solution)/shard_map/all_to_all | solution.py:428
  62.3 1.4 %copy-start = (bf16[128,1280]{1,0:T(8,128)(2,1)}, bf16[128,1280]{1,0:T(8,128)(2,1)S(1)}, u32[]{:S(2)}) copy-start(bf16[128,1280]{1,0:T(8,128)(2,1)S(1)} %collective-permute-done.3.refs_3_) | copy-start | bytes 983044
  62.3 6.4 %collective-permute-start.6 = (bf16[128,1280]{1,0:T(8,128)(2,1)S(1)}, bf16[128,1280]{1,0:T(8,128)(2,1)}, u32[]{:S(2)}, u32[]{:S(2)}) collective-permute-start(bf16[128,1280]{1,0:T(8,128)(2,1)S(1)} %collective-permute-done.3.refs_3_), channel_id=1, source_target_pairs={{0,32},{1,33},{2,34},{3,35},{4,36},{5,37},{6,38},{7,39},{8,232},{9... | collective-permute-start | bytes 983048 | tf_op jit(solution)/shard_map/ppermute | solution.py:392
  62.4 9.7 %collective-permute-start.9 = (bf16[128,1280]{1,0:T(8,128)(2,1)S(1)}, bf16[128,1280]{1,0:T(8,128)(2,1)S(1)}, u32[]{:S(2)}, u32[]{:S(2)}) collective-permute-start(bf16[128,1280]{1,0:T(8,128)(2,1)S(1)} %collective-permute-done.2.after_ref.refs_6_), channel_id=1, source_target_pairs={{0,32},{1,33},{2,34},{3,35},{4,36},{5,37},{6,38},{7,39},{8,232},{9... | collective-permute-start | bytes 983048 | tf_op jit(solution)/shard_map/ppermute | solution.py:392
  68.7 6.9 %collective-permute-start.10 = (bf16[128,1280]{1,0:T(8,128)(2,1)}, bf16[128,1280]{1,0:T(8,128)(2,1)S(1)}, u32[]{:S(2)}, u32[]{:S(2)}) collective-permute-start(bf16[128,1280]{1,0:T(8,128)(2,1)} %collective-permute-done.6.refs_7_), channel_id=1, source_target_pairs={{0,32},{1,33},{2,34},{3,35},{4,36},{5,37},{6,38},{7,39},{8,232},{9... | collective-permute-start | bytes 983048 | tf_op jit(solution)/shard_map/ppermute | solution.py:392
  69.9 7.7 %collective-permute-start.4 = (bf16[128,1280]{1,0:T(8,128)(2,1)S(1)}, bf16[128,1280]{1,0:T(8,128)(2,1)S(1)}, u32[]{:S(2)}, u32[]{:S(2)}) collective-permute-start(bf16[128,1280]{1,0:T(8,128)(2,1)S(1)} %collective-permute-done.1.refs_2_), channel_id=1, source_target_pairs={{0,8},{1,9},{2,10},{3,11},{4,12},{5,13},{6,14},{7,15},{8,0},{9,1},... | collective-permute-start | bytes 983048 | tf_op jit(solution)/shard_map/ppermute | solution.py:392
  71.6 8.8 %collective-permute-start.5 = (bf16[128,1280]{1,0:T(8,128)(2,1)}, bf16[128,1280]{1,0:T(8,128)(2,1)S(1)}, u32[]{:S(2)}, u32[]{:S(2)}) collective-permute-start(bf16[128,1280]{1,0:T(8,128)(2,1)} %copy-done), channel_id=1, source_target_pairs={{0,8},{1,9},{2,10},{3,11},{4,12},{5,13},{6,14},{7,15},{8,0},{9,1},... | collective-permute-start | bytes 983048 | tf_op jit(solution)/shard_map/ppermute | solution.py:392
  71.6 9.6 %collective-permute-start.7 = (bf16[128,1280]{1,0:T(8,128)(2,1)S(1)}, bf16[128,1280]{1,0:T(8,128)(2,1)S(1)}, u32[]{:S(2)}, u32[]{:S(2)}) collective-permute-start(bf16[128,1280]{1,0:T(8,128)(2,1)S(1)} %collective-permute-done.2.after_ref.refs_6_), channel_id=1, source_target_pairs={{0,8},{1,9},{2,10},{3,11},{4,12},{5,13},{6,14},{7,15},{8,0},{9,1},... | collective-permute-start | bytes 983048 | tf_op jit(solution)/shard_map/ppermute | solution.py:392
  72.1 18.7 %collective-permute-start.8 = (bf16[128,1280]{1,0:T(8,128)(2,1)}, bf16[128,1280]{1,0:T(8,128)(2,1)}, u32[]{:S(2)}, u32[]{:S(2)}) collective-permute-start(bf16[128,1280]{1,0:T(8,128)(2,1)} %collective-permute-done.6.refs_7_), channel_id=1, source_target_pairs={{0,8},{1,9},{2,10},{3,11},{4,12},{5,13},{6,14},{7,15},{8,0},{9,1},... | collective-permute-start | bytes 983048 | tf_op jit(solution)/shard_map/ppermute | solution.py:392
  75.7 9.2 %collective-permute-start.13 = (bf16[64,1280]{1,0:T(8,128)(2,1)S(1)}, bf16[64,1280]{1,0:T(8,128)(2,1)S(1)}, u32[]{:S(2)}, u32[]{:S(2)}) collective-permute-start(bf16[64,1280]{1,0:T(8,128)(2,1)S(1)} %slice.36), channel_id=1, source_target_pairs={{0,32},{1,33},{2,34},{3,35},{4,36},{5,37},{6,38},{7,39},{8,232},{9... | collective-permute-start | bytes 491528 | tf_op jit(solution)/shard_map/ppermute | solution.py:392
  77.5 0.7 copy-start.2
  78.2 12.6 %collective-permute-start.11 = (bf16[128,1280]{1,0:T(8,128)(2,1)S(1)}, bf16[128,1280]{1,0:T(8,128)(2,1)}, u32[]{:S(2)}, u32[]{:S(2)}) collective-permute-start(bf16[128,1280]{1,0:T(8,128)(2,1)S(1)} %collective-permute-done.9.refs_10_), channel_id=1, source_target_pairs={{0,8},{1,9},{2,10},{3,11},{4,12},{5,13},{6,14},{7,15},{8,0},{9,1},... | collective-permute-start | bytes 983048 | tf_op jit(solution)/shard_map/ppermute | solution.py:392
  80.5 0.7 copy-start.4
  81.2 9.7 %collective-permute-start.12 = (bf16[128,1280]{1,0:T(8,128)(2,1)S(1)}, bf16[128,1280]{1,0:T(8,128)(2,1)}, u32[]{:S(2)}, u32[]{:S(2)}) collective-permute-start(bf16[128,1280]{1,0:T(8,128)(2,1)S(1)} %collective-permute-done.10.refs_11_), channel_id=1, source_target_pairs={{0,8},{1,9},{2,10},{3,11},{4,12},{5,13},{6,14},{7,15},{8,0},{9,1},... | collective-permute-start | bytes 983048 | tf_op jit(solution)/shard_map/ppermute | solution.py:392
  81.2 0.7 copy-start.6
  81.9 5.2 %collective-permute-start.15 = (bf16[64,1280]{1,0:T(8,128)(2,1)S(1)}, bf16[64,1280]{1,0:T(8,128)(2,1)}, u32[]{:S(2)}, u32[]{:S(2)}) collective-permute-start(bf16[64,1280]{1,0:T(8,128)(2,1)S(1)} %slice.37), channel_id=1, source_target_pairs={{0,32},{1,33},{2,34},{3,35},{4,36},{5,37},{6,38},{7,39},{8,232},{9... | collective-permute-start | bytes 491528 | tf_op jit(solution)/shard_map/ppermute | solution.py:392
  84.9 6.0 %collective-permute-start.14 = (bf16[64,1280]{1,0:T(8,128)(2,1)S(1)}, bf16[64,1280]{1,0:T(8,128)(2,1)}, u32[]{:S(2)}, u32[]{:S(2)}) collective-permute-start(bf16[64,1280]{1,0:T(8,128)(2,1)S(1)} %collective-permute-done.13.refs_14_), channel_id=1, source_target_pairs={{0,8},{1,9},{2,10},{3,11},{4,12},{5,13},{6,14},{7,15},{8,0},{9,1},... | collective-permute-start | bytes 491528 | tf_op jit(solution)/shard_map/ppermute | solution.py:392
  87.1 3.7 %collective-permute-start.16 = (bf16[64,1280]{1,0:T(8,128)(2,1)}, bf16[64,1280]{1,0:T(8,128)(2,1)}, u32[]{:S(2)}, u32[]{:S(2)}) collective-permute-start(bf16[64,1280]{1,0:T(8,128)(2,1)} %collective-permute-done.15.refs_16_), channel_id=1, source_target_pairs={{0,8},{1,9},{2,10},{3,11},{4,12},{5,13},{6,14},{7,15},{8,0},{9,1},... | collective-permute-start | bytes 491528 | tf_op jit(solution)/shard_map/ppermute | solution.py:392
  89.1 1.8 %copy-start.1 = (bf16[128,1280]{1,0:T(8,128)(2,1)S(1)}, bf16[128,1280]{1,0:T(8,128)(2,1)}, u32[]{:S(2)}) copy-start(bf16[128,1280]{1,0:T(8,128)(2,1)} %copy-done) | copy-start | bytes 983044
  89.1 1.8 %copy-start.3 = (bf16[128,1280]{1,0:T(8,128)(2,1)S(1)}, bf16[128,1280]{1,0:T(8,128)(2,1)}, u32[]{:S(2)}) copy-start(bf16[128,1280]{1,0:T(8,128)(2,1)} %copy-done.2) | copy-start | bytes 983044
  89.1 1.8 %copy-start.5 = (bf16[128,1280]{1,0:T(8,128)(2,1)S(1)}, bf16[128,1280]{1,0:T(8,128)(2,1)}, u32[]{:S(2)}) copy-start(bf16[128,1280]{1,0:T(8,128)(2,1)} %copy-done.4) | copy-start | bytes 983044
  89.1 1.8 %copy-start.7 = (bf16[128,1280]{1,0:T(8,128)(2,1)S(1)}, bf16[128,1280]{1,0:T(8,128)(2,1)}, u32[]{:S(2)}) copy-start(bf16[128,1280]{1,0:T(8,128)(2,1)} %copy-done.6) | copy-start | bytes 983044
